TPU v7x, 256 devices: a whole 4x4x8 slice. The times are simulated.
256 devices in a mesh: section: 16 (over x, y_hi, core), fsdp: 16 (over y_lo, z).
Axes of the slice: x: 4, y: 4 (y_hi: 2, y_lo: 2; y = y_hi * 2 + y_lo), z: 8, core: 2. Of those that a mesh axis runs over, the one named last changes fastest.
Arguments:
- text_states: bfloat16 [16, 256, 8192], P('fsdp'), may hold values from -6 to 6
- latents: bfloat16 [16, 512, 8192], P('fsdp', None, 'section'), may hold values from -68 to 68
- norm_gain: float32 [8192], replicated, may hold values from 0.5 to 1.5
- w_query: bfloat16 [8192, 8192], P('fsdp', 'section'), may hold values from -0.0625 to 0.0625
- w_key: bfloat16 [8192, 8192], P('fsdp', 'section'), may hold values from -0.0625 to 0.0625
- w_value: bfloat16 [8192, 8192], P('fsdp', 'section'), may hold values from -0.5 to 0.5
- w_out: bfloat16 [8192, 8192], P('section', 'fsdp'), may hold values from -0.09375 to 0.09375
- xattn_gate: float32 [1], replicated, may hold values from 0.5 to 1.5
- token_image: int32 [16, 256], P('fsdp'), may hold values from -1 to 7, as said below
Outputs:
- mixed_states: bfloat16 [16, 256, 8192], P('fsdp', None, 'section')
Inputs may be any that keep to these rules, and one draw needn't show every extreme that they name: `token_image`: each row never falls from token to token; it is the number of image slots placed at or before the token, minus one.
All inputs are finite; a program needn't handle non-finite values.
Results may differ from a plain program's by a relative error of at most 0.007.
The roundings to bfloat16 on the way count: a program that leaves them out, or rounds other values in their place, can miss the bound.
Values may be sent and summed in bfloat16 or wider, within the bound.
No kernel may reach another device: no remote copies, remote signals or barrier semaphores. Data moves between devices by JAX's collectives and lax.ppermute only.
A program may use at most 128 MiB of HBM per device.

v0:
```python
import jax
import jax.numpy as jnp
from jax import lax
from jax.experimental import pallas as pl
from jax.experimental.pallas import tpu as pltpu
from jax.sharding import PartitionSpec as P

HEAD_DIM = 128
LATENTS = 64
AXES = ("section", "fsdp")
NX, NYH, NC, NYL, NZ = 4, 2, 2, 2, 8


def permute(value, place):
    pairs = []
    for x in range(NX):
        for yh in range(NYH):
            for c in range(NC):
                for yl in range(NYL):
                    for z in range(NZ):
                        tx, tyh, tc, tyl, tz = place(x, yh, c, yl, z)
                        pairs.append(
                            (
                                (x * 4 + yh * 2 + c) * 16 + yl * 8 + z,
                                (tx * 4 + tyh * 2 + tc) * 16 + tyl * 8 + tz,
                            )
                        )
    return lax.ppermute(value, AXES, pairs)


def to_parity(value):
    return permute(value, lambda x, yh, c, yl, z: (x, yh, z % 2, c, z ^ yl ^ c))


def swap_core_parity(value):
    return permute(value, lambda x, yh, c, yl, z: (x, yh, z % 2, yl, z // 2 * 2 + c))


def swap_cores(value):
    return permute(value, lambda x, yh, c, yl, z: (x, yh, 1 - c, yl, z))


def over_x(value, r):
    return permute(value, lambda x, yh, c, yl, z: (x ^ r, yh, c, yl, z))


def along_x(value, step):
    return permute(value, lambda x, yh, c, yl, z: ((x + step) % NX, yh, c, yl, z))


def over_y(value, q):
    return permute(value, lambda x, yh, c, yl, z: (x, yh ^ (q >> 1), c, yl ^ (q & 1), z))


def gather_z(value):
    groups = [list(range(NZ)), list(range(NZ, 2 * NZ))]
    return lax.all_gather(value, "fsdp", axis=0, axis_index_groups=groups)


def after(value, *earlier):
    return lax.optimization_barrier((value, *earlier))[0]


def gather_y(block):
    return jnp.stack([block] + [over_y(block, q) for q in (1, 2, 3)])


def gather_x(column):
    up, down = along_x(column, 1), along_x(column, -1)
    far = [along_x(up[:2], 1), along_x(down[2:], -1)]
    return jnp.concatenate([column, up, *far, down], axis=0)


def query_kernel(place_ref, own_ref, other_ref, weight_ref, kept, sent):
    @pl.when(pl.program_id(0) == 0)
    def _():
        kept[...] = jnp.zeros_like(kept)
        sent[...] = jnp.zeros_like(sent)

    weight = weight_ref[...]
    own = jnp.dot(own_ref[...], weight, preferred_element_type=jnp.float32)
    other = jnp.dot(other_ref[...], weight, preferred_element_type=jnp.float32)
    stays = place_ref[2] == place_ref[3]
    kept[...] += jnp.where(stays, own, other)
    sent[...] += jnp.where(stays, other, own)


def latent_kernel(place_ref, mine_ref, theirs_ref, weight_ref, kept, sent):
    @pl.when(pl.program_id(0) == 0)
    def _():
        kept[...] = jnp.zeros_like(kept)
        sent[...] = jnp.zeros_like(sent)

    for out, latent_ref in ((kept, mine_ref), (sent, theirs_ref)):
        latent = latent_ref[...]
        for n in range(2):
            out[n] += jnp.dot(latent, weight_ref[n], preferred_element_type=jnp.float32)


def weight_at(s, p):
    return s // 2 * 2 + ((s % 2) ^ p[2] ^ p[3])


def project_queries(place, normed, other_half, weights):
    length = normed.shape[0]
    steps, depth, width = weights.shape
    out = jax.ShapeDtypeStruct((length, width), jnp.float32)
    whole = pl.BlockSpec((length, width), lambda s, p: (0, 0))
    return pl.pallas_call(
        query_kernel,
        out_shape=(out, out),
        grid_spec=pltpu.PrefetchScalarGridSpec(
            num_scalar_prefetch=1,
            grid=(steps,),
            in_specs=[
                pl.BlockSpec((length, depth), lambda s, p: (0, (s % 2) * 8 + (s // 2) * 2 + p[2])),
                pl.BlockSpec((length, depth), lambda s, p: (0, (s % 2) * 4 + s // 2)),
                pl.BlockSpec((None, depth, width), lambda s, p: (weight_at(s, p), 0, 0)),
            ],
            out_specs=(whole, whole),
        ),
        compiler_params=pltpu.CompilerParams(vmem_limit_bytes=32 * 2**20),
        cost_estimate=pl.CostEstimate(
            flops=4 * length * steps * depth * width,
            bytes_accessed=2 * steps * depth * (2 * length + width) + 8 * length * width,
            transcendentals=0,
        ),
    )(place, normed, other_half, weights)


def project_latents(place, latent_blocks, weights):
    key_count = latent_blocks.shape[1]
    steps, kinds, depth, width = weights.shape

    def latent_spec(flip):
        def index(s, p):
            x_at, y_at = (s % 2) * 2 + s // 4, ((s // 2) % 2) * 2 + (p[2] + flip) % 2
            return (((p[0] - x_at + NX) % NX) * 4 + (y_at ^ p[1]), 0, 0)

        return pl.BlockSpec((None, key_count, depth), index)

    out = jax.ShapeDtypeStruct((kinds, key_count, width), jnp.float32)
    whole = pl.BlockSpec((kinds, key_count, width), lambda s, p: (0, 0, 0))
    return pl.pallas_call(
        latent_kernel,
        out_shape=(out, out),
        grid_spec=pltpu.PrefetchScalarGridSpec(
            num_scalar_prefetch=1,
            grid=(steps,),
            in_specs=[
                latent_spec(0),
                latent_spec(1),
                pl.BlockSpec((None, kinds, depth, width), lambda s, p: (weight_at(s, p), 0, 0, 0)),
            ],
            out_specs=(whole, whole),
        ),
        compiler_params=pltpu.CompilerParams(vmem_limit_bytes=40 * 2**20),
        cost_estimate=pl.CostEstimate(
            flops=4 * kinds * key_count * steps * depth * width,
            bytes_accessed=2 * steps * depth * (2 * key_count + kinds * width)
            + 8 * kinds * key_count * width,
            transcendentals=0,
        ),
    )(place, latent_blocks, latent_blocks, weights)


def out_kernel(place_ref, mine_ref, theirs_ref, block_ref, *parts):
    core, y_low, x_high = place_ref[2], place_ref[3], place_ref[0] // 2

    def product(ref):
        return (
            jnp.dot(ref[0], block_ref[y_low], preferred_element_type=jnp.float32)
            + jnp.dot(ref[1], block_ref[1 - y_low], preferred_element_type=jnp.float32)
        ).astype(jnp.bfloat16)

    mine, theirs = product(mine_ref), product(theirs_ref)
    near = jnp.where(core == x_high, mine, theirs)
    far = jnp.where(core == x_high, theirs, mine)
    for n in range(2):

        @pl.when(pl.program_id(0) // 2 == n)
        def _():
            parts[n][...] = near
            parts[2 + n][...] = far


def partial_sums(place, mine, theirs, blocks):
    _, length, depth = mine.shape
    steps, width = blocks.shape[0] // 2, blocks.shape[2]
    rows = pl.BlockSpec((2, length, depth), lambda s, p: (0, 0, 0))

    def block_index(s, p):
        return (((s // 2) ^ (p[0] % 2)) * 2 + ((s % 2) ^ (p[1] // 2)), 0, 0)

    def out_spec(n):
        def index(s, p):
            return (jnp.where(s // 2 == n, s % 2, jnp.where(s // 2 < n, 0, 1)), 0, 0)

        return pl.BlockSpec((None, length, width), index)

    return pl.pallas_call(
        out_kernel,
        out_shape=[jax.ShapeDtypeStruct((2, length, width), jnp.bfloat16)] * 4,
        grid_spec=pltpu.PrefetchScalarGridSpec(
            num_scalar_prefetch=1,
            grid=(steps,),
            in_specs=[rows, rows, pl.BlockSpec((2, depth, width), block_index)],
            out_specs=[out_spec(n % 2) for n in range(4)],
        ),
        compiler_params=pltpu.CompilerParams(vmem_limit_bytes=32 * 2**20),
        cost_estimate=pl.CostEstimate(
            flops=8 * length * depth * steps * width,
            bytes_accessed=2 * (4 * length * depth + 2 * steps * depth * width + 8 * length * width),
            transcendentals=0,
        ),
    )(place, mine, theirs, blocks)


def layer_norm(text_rows, norm_gain):
    values = text_rows.astype(jnp.float32)
    center = jnp.mean(values, axis=-1, keepdims=True)
    spread = jnp.mean(jnp.square(values - center), axis=-1, keepdims=True)
    return ((values - center) * lax.rsqrt(spread + 1e-05) * norm_gain).astype(jnp.bfloat16)


def attention_weights(queries, keys, token_image):
    length, head_width = queries.shape
    key_count = keys.shape[0]
    head_count = head_width // HEAD_DIM
    query_heads = queries.reshape(length, head_count, HEAD_DIM)
    key_heads = keys.reshape(key_count, head_count, HEAD_DIM)
    scores = jnp.einsum(
        "lhd,rhd->hlr", query_heads, key_heads, preferred_element_type=jnp.float32
    ) * HEAD_DIM ** (-0.5)
    blocks = lax.broadcasted_iota(jnp.int32, (key_count,), 0) // LATENTS
    visible = (blocks[None, :] <= token_image[:, None])[None, :, :]
    masked = jnp.where(visible, scores, -1e30)
    row_top = jnp.max(masked, axis=-1, keepdims=True)
    has_image = jnp.any(visible, axis=-1, keepdims=True)
    row_top = jnp.where(has_image, row_top, 0.0)
    exp_terms = jnp.where(visible, jnp.exp(masked - row_top), 0.0)
    denominator = jnp.sum(exp_terms, axis=-1, keepdims=True)
    return (exp_terms / jnp.maximum(denominator, 1.0)).astype(jnp.bfloat16)


def attend(weights, values):
    key_count, head_width = values.shape
    value_heads = values.reshape(key_count, head_width // HEAD_DIM, HEAD_DIM)
    attended = jnp.einsum("hlr,rhd->lhd", weights, value_heads, preferred_element_type=jnp.float32)
    return attended.astype(jnp.bfloat16).reshape(-1, head_width)


def to_final(piece, g):
    return permute(piece, lambda x, yh, c, yl, z: (yl * 2 + x % 2, yh ^ g, c, x // 2, z))


def total(own, moved):
    result = own.astype(jnp.float32)
    for part in moved:
        result = result + part.astype(jnp.float32)
    return result


def body(text_states, latents, norm_gain, w_query, w_key, w_value, w_out, xattn_gate, token_image):
    _, length, model_width = text_states.shape
    key_count = latents.shape[1]
    width = w_out.shape[1]
    section, place = lax.axis_index("section"), lax.axis_index("fsdp")
    x, yh, core, yl = section // 4, (section // 2) % 2, section % 2, place // NZ
    here = jnp.stack([x, yh * 2 + yl, core, yl]).astype(jnp.int32)

    latent_shard = to_parity(jnp.stack([w_key, w_value]))
    latent_weights = gather_z(latent_shard)
    column = gather_y(latents[0])
    latent_blocks = gather_x(column)
    query_shard = to_parity(after(w_query, column, latent_shard))
    query_weights = gather_z(query_shard)

    normed = layer_norm(text_states[0], norm_gain)
    own_half = jnp.concatenate(
        [lax.dynamic_slice_in_dim(normed, (2 * n + core) * width, width, 1) for n in range(NZ)], axis=1
    )
    other_half = over_y(after(own_half, query_shard), 1)
    out_shard = swap_core_parity(after(w_out, query_shard))
    out_blocks = gather_z(out_shard)
    other_image = over_y(after(token_image, out_shard), 1)
    images = jnp.where(core == yl, token_image, other_image)[0]

    kept, sent = project_queries(here, normed, other_half, query_weights)
    queries = (kept + swap_cores(sent)).astype(jnp.bfloat16)
    kept, sent = project_latents(here, latent_blocks, latent_weights)
    keys, values = (kept + swap_cores(sent)).astype(jnp.bfloat16)
    attended = attend(attention_weights(queries, keys, images), values)

    mine = jnp.stack([attended, over_y(attended, 1)])
    parts = partial_sums(here, mine, swap_cores(mine), out_blocks)
    near = total(parts[0], [over_x(parts[r], r) for r in (1, 2, 3)]).astype(jnp.bfloat16)
    projected = total(to_final(near[0], 0), [to_final(near[1], 1)])
    own_text = lax.dynamic_slice_in_dim(text_states[0], section * width, width, 1)
    mixed = own_text.astype(jnp.float32) + jnp.tanh(xattn_gate[0]) * projected
    return mixed.astype(jnp.bfloat16)[None]


def solution(mesh):
    in_specs = (
        P("fsdp", None, None),
        P("fsdp", None, "section"),
        P(),
        P("fsdp", "section"),
        P("fsdp", "section"),
        P("fsdp", "section"),
        P("section", "fsdp"),
        P(),
        P("fsdp", None),
    )
    out_specs = P("fsdp", None, "section")
    return jax.shard_map(body, mesh=mesh, in_specs=in_specs, out_specs=out_specs, check_vma=False)
```

profile of v0, /device:TPU:8, one launch (start us, length us, event | category | flops | bytes accessed | tf_op | source)
XLA Modules:
  0.0 306.3 jit_solution(13366311895992100299)
XLA Ops:
  7.9 3.7 %collective-permute-start.7 = (bf16[2,512,512]{2,1,0:T(8,128)(2,1)S(1)}, bf16[2,512,512]{2,1,0:T(8,128)(2,1)S(1)}, u32[]{:S(2)}, u32[]{:S(2)}) collective-permute-start(bf16[2,512,512]{2,1,0:T(8,128)(2,1)S(1)} %pad_maximum_fusion.1), channel_id=1, source_target_pairs={{0,0},{1,17},{2,2},{3,19},{4,4},{5,21},{6,6},{7,23},{8,1},{9,16},{... | collective-permute-start | bytes 3145736 | tf_op jit(solution)/shard_map/ppermute | solution.py:28
  11.6 12.3 %collective-permute-done.7 = bf16[2,512,512]{2,1,0:T(8,128)(2,1)S(1)} collective-permute-done((bf16[2,512,512]{2,1,0:T(8,128)(2,1)S(1)}, bf16[2,512,512]{2,1,0:T(8,128)(2,1)S(1)}, u32[]{:S(2)}, u32[]{:S(2)}) %collective-permute-start.7) | collective-permute-done | bytes 1048608 | tf_op jit(solution)/shard_map/ppermute | solution.py:28
  28.5 11.3 %collective-permute-done = bf16[512,512]{1,0:T(8,128)(2,1)S(1)} collective-permute-done((bf16[512,512]{1,0:T(8,128)(2,1)S(1)}, bf16[512,512]{1,0:T(8,128)(2,1)S(1)}, u32[]{:S(2)}, u32[]{:S(2)}) %collective-permute-start) | collective-permute-done | bytes 524320 | tf_op jit(solution)/shard_map/ppermute | solution.py:28
  39.8 11.4 %collective-permute-done.1 = bf16[512,512]{1,0:T(8,128)(2,1)S(1)} collective-permute-done((bf16[512,512]{1,0:T(8,128)(2,1)S(1)}, bf16[512,512]{1,0:T(8,128)(2,1)S(1)}, u32[]{:S(2)}, u32[]{:S(2)}) %collective-permute-start.1) | collective-permute-done | bytes 524320 | tf_op jit(solution)/shard_map/ppermute | solution.py:28
  57.6 17.9 %collective-permute-done.9 = bf16[512,512]{1,0:T(8,128)(2,1)S(1)} collective-permute-done((bf16[512,512]{1,0:T(8,128)(2,1)S(1)}, bf16[512,512]{1,0:T(8,128)(2,1)S(1)}, u32[]{:S(2)}, u32[]{:S(2)}) %collective-permute-start.9) | collective-permute-done | bytes 524320 | tf_op jit(solution)/shard_map/ppermute | solution.py:28
  76.4 3.0 convert_reduce_fusion
  84.5 3.7 %fusion.5.own_ref = bf16[256,8192]{1,0:T(8,128)(2,1)} fusion(bf16[1,256,8192]{2,1,0:T(8,128)(2,1)S(1)} %copy-done.4, f32[8192]{0:T(1024)S(1)} %copy-done.11, f32[256]{0:T(256)S(1)} %add_rsqrt_fusion, f32[256]{0:T(256)S(1)} %broadcast_multiply_fusion), kind=kLoop, calls=%fused_computation.7 | loop fusion | flops 10485760 | bytes 8423424 | tf_op jit(solution)/shard_map/convert_element_type | solution.py:223
  95.0 5.4 %collective-permute-start.10 = (bf16[512,512]{1,0:T(8,128)(2,1)}, bf16[512,512]{1,0:T(8,128)(2,1)}, u32[]{:S(2)}, u32[]{:S(2)}) collective-permute-start(bf16[512,512]{1,0:T(8,128)(2,1)} %param.15), channel_id=1, source_target_pairs={{0,0},{1,16},{2,2},{3,18},{4,4},{5,20},{6,6},{7,22},{8,8},{9,24},{... | collective-permute-start | bytes 1572872 | tf_op jit(solution)/shard_map/ppermute | solution.py:28
  106.4 23.4 %collective-permute-done.3 = bf16[4,512,512]{2,1,0:T(8,128)(2,1)} collective-permute-done((bf16[4,512,512]{2,1,0:T(8,128)(2,1)}, bf16[4,512,512]{2,1,0:T(8,128)(2,1)}, u32[]{:S(2)}, u32[]{:S(2)}) %collective-permute-start.3) | collective-permute-done | bytes 2097184 | tf_op jit(solution)/shard_map/ppermute | solution.py:28
  134.2 3.0 collective-permute-start.6
  140.8 3.1 %constant_dynamic-update-slice_fusion.3 = bf16[16,512,512]{2,1,0:T(8,128)(2,1)} fusion(bf16[16,512,512]{2,1,0:T(8,128)(2,1)} %constant_dynamic-update-slice_fusion.4, bf16[4,512,512]{2,1,0:T(8,128)(2,1)} %collective-permute-done.3), kind=kLoop, calls=%fused_computation.44 | loop fusion | bytes 4194304
  143.9 15.4 %collective-permute-done.4 = bf16[2,512,512]{2,1,0:T(8,128)(2,1)} collective-permute-done((bf16[2,512,512]{2,1,0:T(8,128)(2,1)}, bf16[2,512,512]{2,1,0:T(8,128)(2,1)}, u32[]{:S(2)}, u32[]{:S(2)}) %collective-permute-start.4) | collective-permute-done | bytes 1048608 | tf_op jit(solution)/shard_map/ppermute | solution.py:28
  164.1 3.5 %copy-done.2 = bf16[16,512,512]{2,1,0:T(8,128)(2,1)S(1)} copy-done((bf16[16,512,512]{2,1,0:T(8,128)(2,1)S(1)}, bf16[16,512,512]{2,1,0:T(8,128)(2,1)}, u32[]{:S(2)}) %copy-start.2) | copy-done | bytes 8388632
  167.6 13.8 %shard_map.91 = (f32[2,512,512]{2,1,0:T(8,128)S(1)}, f32[2,512,512]{2,1,0:T(8,128)}) custom-call(s32[4]{0:T(128)S(1)} %pad_add_fusion.place_ref, bf16[16,512,512]{2,1,0:T(8,128)(2,1)S(1)} %copy-done.2, bf16[16,512,512]{2,1,0:T(8,128)(2,1)S(1)} %copy-done.2, bf16[8,2,512,512]{3,2,1,0:T(8,128)(2,1)} %bitcast.74), custom_call_target="tpu_custom_call" | custom-call | flops 8589934592 | bytes 20971520 | tf_op jit(solution)/shard_map/pallas_call | solution.py:144
  181.8 7.6 %collective-permute-done.11 = s32[1,256]{1,0:T(1,128)S(1)} collective-permute-done((s32[1,256]{1,0:T(1,128)S(1)}, s32[1,256]{1,0:T(1,128)S(1)}, u32[]{:S(2)}, u32[]{:S(2)}) %collective-permute-start.11) | collective-permute-done | bytes 1056 | tf_op jit(solution)/shard_map/ppermute | solution.py:28
  194.2 7.1 %shard_map.92 = (f32[256,512]{1,0:T(8,128)S(1)}, f32[256,512]{1,0:T(8,128)S(1)}) custom-call(s32[4]{0:T(128)S(1)} %pad_add_fusion.place_ref, bf16[256,8192]{1,0:T(8,128)(2,1)S(1)} %copy-done, bf16[256,4096]{1,0:T(8,128)(2,1)} %collective-permute-done.12.other_ref, bf16[8,512,512]{2,1,0:T(8,128)(2,1)S(1)} %bitcast.58), custom_call_target="tpu_custom_call" | custom-call | flops 2147483648 | bytes 9437184 | tf_op jit(solution)/shard_map/pallas_call | solution.py:109
  208.2 8.0 %collective-permute-done.14 = bf16[256,512]{1,0:T(8,128)(2,1)S(1)} collective-permute-done((bf16[256,512]{1,0:T(8,128)(2,1)S(1)}, bf16[256,512]{1,0:T(8,128)(2,1)S(1)}, u32[]{:S(2)}, u32[]{:S(2)}) %collective-permute-start.14) | collective-permute-done | bytes 262176 | tf_op jit(solution)/shard_map/ppermute | solution.py:28
  216.3 28.6 %all-gather.11.cloned.1.call-done = bf16[4096,512]{1,0:T(8,128)(2,1)} async-done(((bf16[512,512]{1,0:T(8,128)(2,1)}), bf16[4096,512]{1,0:T(8,128)(2,1)}) %all-gather.11.cloned.1.call-update) | async-done | bytes 4194320 | tf_op jit(solution)/shard_map/all_gather | solution.py:57
  247.1 3.6 %shard_map.93 = (bf16[2,256,512]{2,1,0:T(8,128)(2,1)S(1)}, bf16[2,256,512]{2,1,0:T(8,128)(2,1)S(1)}, bf16[2,256,512]{2,1,0:T(8,128)(2,1)S(1)}, bf16[2,256,512]{2,1,0:T(8,128)(2,1)S(1)}) custom-call(s32[4]{0:T(128)S(1)} %pad_add_fusion.place_ref, bf16[2,256,512]{2,1,0:T(8,128)(2,1)S(1)} %pad_maximum_fusion.2.mine_ref, ...), custom_call_target="tpu_custom_call" | custom-call | flops 2147483648 | bytes 7340032 | tf_op jit(solution)/shard_map/pallas_call | solution.py:201
  255.6 10.1 %collective-permute-done.16 = bf16[2,256,512]{2,1,0:T(8,128)(2,1)S(1)} collective-permute-done((bf16[2,256,512]{2,1,0:T(8,128)(2,1)S(1)}, bf16[2,256,512]{2,1,0:T(8,128)(2,1)S(1)}, u32[]{:S(2)}, u32[]{:S(2)}) %collective-permute-start.16) | collective-permute-done | bytes 524320 | tf_op jit(solution)/shard_map/ppermute | solution.py:28
  265.7 12.3 %collective-permute-done.17 = bf16[2,256,512]{2,1,0:T(8,128)(2,1)S(1)} collective-permute-done((bf16[2,256,512]{2,1,0:T(8,128)(2,1)S(1)}, bf16[2,256,512]{2,1,0:T(8,128)(2,1)S(1)}, u32[]{:S(2)}, u32[]{:S(2)}) %collective-permute-start.17) | collective-permute-done | bytes 524320 | tf_op jit(solution)/shard_map/ppermute | solution.py:28
  282.8 5.2 %collective-permute-start.20 = (bf16[256,512]{1,0:T(8,128)(2,1)S(1)}, bf16[256,512]{1,0:T(8,128)(2,1)S(1)}, u32[]{:S(2)}, u32[]{:S(2)}) collective-permute-start(bf16[256,512]{1,0:T(8,128)(2,1)S(1)} %get-tuple-element.32), channel_id=1, source_target_pairs={{0,32},{1,33},{2,34},{3,35},{4,36},{5,37},{6,38},{7,39},{8,160},{9... | collective-permute-start | bytes 786440 | tf_op jit(solution)/shard_map/ppermute | solution.py:28
  288.7 5.8 %collective-permute-done.19 = bf16[256,512]{1,0:T(8,128)(2,1)S(1)} collective-permute-done((bf16[256,512]{1,0:T(8,128)(2,1)S(1)}, bf16[256,512]{1,0:T(8,128)(2,1)S(1)}, u32[]{:S(2)}, u32[]{:S(2)}) %collective-permute-start.19) | collective-permute-done | bytes 262176 | tf_op jit(solution)/shard_map/ppermute | solution.py:28
  294.5 3.6 %collective-permute-done.20 = bf16[256,512]{1,0:T(8,128)(2,1)S(1)} collective-permute-done((bf16[256,512]{1,0:T(8,128)(2,1)S(1)}, bf16[256,512]{1,0:T(8,128)(2,1)S(1)}, u32[]{:S(2)}, u32[]{:S(2)}) %collective-permute-start.20) | collective-permute-done | bytes 262176 | tf_op jit(solution)/shard_map/ppermute | solution.py:28
  (103 shorter events, 69.5 us)
Async XLA Ops:
  6.5 157.5 %all-gather.7.cloned.1.call-start = ((), (), s32[]{:S(2)}) async-start(), calls=%async_computation | async-start | bytes 9437184 | tf_op jit(solution)/shard_map/all_gather | solution.py:57
  7.9 16.0 %collective-permute-start.7 = (bf16[2,512,512]{2,1,0:T(8,128)(2,1)S(1)}, bf16[2,512,512]{2,1,0:T(8,128)(2,1)S(1)}, u32[]{:S(2)}, u32[]{:S(2)}) collective-permute-start(bf16[2,512,512]{2,1,0:T(8,128)(2,1)S(1)} %pad_maximum_fusion.1), channel_id=1, source_target_pairs={{0,0},{1,17},{2,2},{3,19},{4,4},{5,21},{6,6},{7,23},{8,1},{9,16},{... | collective-permute-start | bytes 3145736 | tf_op jit(solution)/shard_map/ppermute | solution.py:28
  24.9 164.9 %all-gather.9.cloned.1.call-start = ((), (), s32[]{:S(2)}) async-start(), calls=%async_computation.1 | async-start | bytes 4718592 | tf_op jit(solution)/shard_map/all_gather | solution.py:57
  25.0 14.8 %collective-permute-start = (bf16[512,512]{1,0:T(8,128)(2,1)S(1)}, bf16[512,512]{1,0:T(8,128)(2,1)S(1)}, u32[]{:S(2)}, u32[]{:S(2)}) collective-permute-start(bf16[512,512]{1,0:T(8,128)(2,1)S(1)} %bitcast.60), channel_id=1, source_target_pairs={{0,8},{1,9},{2,10},{3,11},{4,12},{5,13},{6,14},{7,15},{8,0},{9,1},... | collective-permute-start | bytes 1572872 | tf_op jit(solution)/shard_map/ppermute | solution.py:28
  25.1 26.2 %collective-permute-start.1 = (bf16[512,512]{1,0:T(8,128)(2,1)S(1)}, bf16[512,512]{1,0:T(8,128)(2,1)S(1)}, u32[]{:S(2)}, u32[]{:S(2)}) collective-permute-start(bf16[512,512]{1,0:T(8,128)(2,1)S(1)} %bitcast.61), channel_id=1, source_target_pairs={{0,32},{1,33},{2,34},{3,35},{4,36},{5,37},{6,38},{7,39},{8,40},{9,... | collective-permute-start | bytes 1572872 | tf_op jit(solution)/shard_map/ppermute | solution.py:28
  27.7 26.0 %collective-permute-start.2 = (bf16[512,512]{1,0:T(8,128)(2,1)S(1)}, bf16[512,512]{1,0:T(8,128)(2,1)S(1)}, u32[]{:S(2)}, u32[]{:S(2)}) collective-permute-start(bf16[512,512]{1,0:T(8,128)(2,1)S(1)} %bitcast.62), channel_id=1, source_target_pairs={{0,40},{1,41},{2,42},{3,43},{4,44},{5,45},{6,46},{7,47},{8,32},{9,... | collective-permute-start | bytes 1572872 | tf_op jit(solution)/shard_map/ppermute | solution.py:28
  55.3 20.2 %collective-permute-start.9 = (bf16[512,512]{1,0:T(8,128)(2,1)S(1)}, bf16[512,512]{1,0:T(8,128)(2,1)S(1)}, u32[]{:S(2)}, u32[]{:S(2)}) collective-permute-start(bf16[512,512]{1,0:T(8,128)(2,1)S(1)} %copy-done.13), channel_id=1, source_target_pairs={{0,0},{1,17},{2,2},{3,19},{4,4},{5,21},{6,6},{7,23},{8,1},{9,16},{... | collective-permute-start | bytes 1572872 | tf_op jit(solution)/shard_map/ppermute | solution.py:28
  76.3 168.6 %all-gather.11.cloned.1.call-start = ((), (), s32[]{:S(2)}) async-start(), calls=%async_computation.2 | async-start | bytes 4718592 | tf_op jit(solution)/shard_map/all_gather | solution.py:57
  81.1 48.6 %collective-permute-start.3 = (bf16[4,512,512]{2,1,0:T(8,128)(2,1)}, bf16[4,512,512]{2,1,0:T(8,128)(2,1)}, u32[]{:S(2)}, u32[]{:S(2)}) collective-permute-start(bf16[4,512,512]{2,1,0:T(8,128)(2,1)} %pad_maximum_fusion), channel_id=1, source_target_pairs={{0,64},{1,65},{2,66},{3,67},{4,68},{5,69},{6,70},{7,71},{8,72},{9,... | collective-permute-start | bytes 6291464 | tf_op jit(solution)/shard_map/ppermute | solution.py:28
  82.7 51.4 %collective-permute-start.5 = (bf16[4,512,512]{2,1,0:T(8,128)(2,1)}, bf16[4,512,512]{2,1,0:T(8,128)(2,1)S(1)}, u32[]{:S(2)}, u32[]{:S(2)}) collective-permute-start(bf16[4,512,512]{2,1,0:T(8,128)(2,1)} %pad_maximum_fusion), channel_id=1, source_target_pairs={{0,192},{1,193},{2,194},{3,195},{4,196},{5,197},{6,198},{7,199},{8... | collective-permute-start | bytes 6291464 | tf_op jit(solution)/shard_map/ppermute | solution.py:28
  95.0 39.0 %collective-permute-start.10 = (bf16[512,512]{1,0:T(8,128)(2,1)}, bf16[512,512]{1,0:T(8,128)(2,1)}, u32[]{:S(2)}, u32[]{:S(2)}) collective-permute-start(bf16[512,512]{1,0:T(8,128)(2,1)} %param.15), channel_id=1, source_target_pairs={{0,0},{1,16},{2,2},{3,18},{4,4},{5,20},{6,6},{7,22},{8,8},{9,24},{... | collective-permute-start | bytes 1572872 | tf_op jit(solution)/shard_map/ppermute | solution.py:28
  132.1 27.2 %collective-permute-start.4 = (bf16[2,512,512]{2,1,0:T(8,128)(2,1)}, bf16[2,512,512]{2,1,0:T(8,128)(2,1)}, u32[]{:S(2)}, u32[]{:S(2)}) collective-permute-start(bf16[2,512,512]{2,1,0:T(8,128)(2,1)} %slice.16), channel_id=1, source_target_pairs={{0,64},{1,65},{2,66},{3,67},{4,68},{5,69},{6,70},{7,71},{8,72},{9,... | collective-permute-start | bytes 3145736 | tf_op jit(solution)/shard_map/ppermute | solution.py:28
  134.2 27.4 %collective-permute-start.6 = (bf16[2,512,512]{2,1,0:T(8,128)(2,1)S(1)}, bf16[2,512,512]{2,1,0:T(8,128)(2,1)S(1)}, u32[]{:S(2)}, u32[]{:S(2)}) collective-permute-start(bf16[2,512,512]{2,1,0:T(8,128)(2,1)S(1)} %slice.17), channel_id=1, source_target_pairs={{0,192},{1,193},{2,194},{3,195},{4,196},{5,197},{6,198},{7,199},{8... | collective-permute-start | bytes 3145736 | tf_op jit(solution)/shard_map/ppermute | solution.py:28
  140.8 49.0 %collective-permute-start.12 = (bf16[256,4096]{1,0:T(8,128)(2,1)}, bf16[256,4096]{1,0:T(8,128)(2,1)}, u32[]{:S(2)}, u32[]{:S(2)}) collective-permute-start(bf16[256,4096]{1,0:T(8,128)(2,1)} %dynamic-slice_dynamic-update-slice_fusion), channel_id=1, source_target_pairs={{0,8},{1,9},{2,10},{3,11},{4,12},{5,13},{6,14},{7,15},{8,0},{9,1},... | collective-permute-start | bytes 6291464 | tf_op jit(solution)/shard_map/ppermute | solution.py:28
  181.3 20.1 %collective-permute-start.8 = (f32[2,512,512]{2,1,0:T(8,128)}, f32[2,512,512]{2,1,0:T(8,128)}, u32[]{:S(2)}, u32[]{:S(2)}) collective-permute-start(f32[2,512,512]{2,1,0:T(8,128)} %get-tuple-element.18), channel_id=1, source_target_pairs={{0,16},{1,17},{2,18},{3,19},{4,20},{5,21},{6,22},{7,23},{8,24},{9,... | collective-permute-start | bytes 6291464 | tf_op jit(solution)/shard_map/ppermute | solution.py:28
  181.8 7.6 %collective-permute-start.11 = (s32[1,256]{1,0:T(1,128)S(1)}, s32[1,256]{1,0:T(1,128)S(1)}, u32[]{:S(2)}, u32[]{:S(2)}) collective-permute-start(s32[1,256]{1,0:T(1,128)S(1)} %copy-done.12), channel_id=1, source_target_pairs={{0,8},{1,9},{2,10},{3,11},{4,12},{5,13},{6,14},{7,15},{8,0},{9,1},... | collective-permute-start | bytes 3080 | tf_op jit(solution)/shard_map/ppermute | solution.py:28
  201.3 2.5 collective-permute-start.13
  207.4 8.8 %collective-permute-start.14 = (bf16[256,512]{1,0:T(8,128)(2,1)S(1)}, bf16[256,512]{1,0:T(8,128)(2,1)S(1)}, u32[]{:S(2)}, u32[]{:S(2)}) collective-permute-start(bf16[256,512]{1,0:T(8,128)(2,1)S(1)} %copy.27), channel_id=1, source_target_pairs={{0,8},{1,9},{2,10},{3,11},{4,12},{5,13},{6,14},{7,15},{8,0},{9,1},... | collective-permute-start | bytes 786440 | tf_op jit(solution)/shard_map/ppermute | solution.py:28
  216.2 28.7 %collective-permute-start.15 = (bf16[2,256,512]{2,1,0:T(8,128)(2,1)S(1)}, bf16[2,256,512]{2,1,0:T(8,128)(2,1)S(1)}, u32[]{:S(2)}, u32[]{:S(2)}) collective-permute-start(bf16[2,256,512]{2,1,0:T(8,128)(2,1)S(1)} %pad_maximum_fusion.2.mine_ref), channel_id=1, source_target_pairs={{0,16},{1,17},{2,18},{3,19},{4,20},{5,21},{6,22},{7,23},{8,24},{9,... | collective-permute-start | bytes 1572872 | tf_op jit(solution)/shard_map/ppermute | solution.py:28
  250.8 14.9 %collective-permute-start.16 = (bf16[2,256,512]{2,1,0:T(8,128)(2,1)S(1)}, bf16[2,256,512]{2,1,0:T(8,128)(2,1)S(1)}, u32[]{:S(2)}, u32[]{:S(2)}) collective-permute-start(bf16[2,256,512]{2,1,0:T(8,128)(2,1)S(1)} %get-tuple-element.26), channel_id=1, source_target_pairs={{0,64},{1,65},{2,66},{3,67},{4,68},{5,69},{6,70},{7,71},{8,72},{9,... | collective-permute-start | bytes 1572872 | tf_op jit(solution)/shard_map/ppermute | solution.py:28
  252.3 25.7 %collective-permute-start.17 = (bf16[2,256,512]{2,1,0:T(8,128)(2,1)S(1)}, bf16[2,256,512]{2,1,0:T(8,128)(2,1)S(1)}, u32[]{:S(2)}, u32[]{:S(2)}) collective-permute-start(bf16[2,256,512]{2,1,0:T(8,128)(2,1)S(1)} %get-tuple-element.27), channel_id=1, source_target_pairs={{0,128},{1,129},{2,130},{3,131},{4,132},{5,133},{6,134},{7,135},{8... | collective-permute-start | bytes 1572872 | tf_op jit(solution)/shard_map/ppermute | solution.py:28
  255.0 25.6 %collective-permute-start.18 = (bf16[2,256,512]{2,1,0:T(8,128)(2,1)S(1)}, bf16[2,256,512]{2,1,0:T(8,128)(2,1)S(1)}, u32[]{:S(2)}, u32[]{:S(2)}) collective-permute-start(bf16[2,256,512]{2,1,0:T(8,128)(2,1)S(1)} %get-tuple-element.28), channel_id=1, source_target_pairs={{0,192},{1,193},{2,194},{3,195},{4,196},{5,197},{6,198},{7,199},{8... | collective-permute-start | bytes 1572872 | tf_op jit(solution)/shard_map/ppermute | solution.py:28
  280.9 13.6 %collective-permute-start.19 = (bf16[256,512]{1,0:T(8,128)(2,1)S(1)}, bf16[256,512]{1,0:T(8,128)(2,1)S(1)}, u32[]{:S(2)}, u32[]{:S(2)}) collective-permute-start(bf16[256,512]{1,0:T(8,128)(2,1)S(1)} %get-tuple-element.31), channel_id=1, source_target_pairs={{0,0},{1,1},{2,2},{3,3},{4,4},{5,5},{6,6},{7,7},{8,128},{9,129},{1... | collective-permute-start | bytes 786440 | tf_op jit(solution)/shard_map/ppermute | solution.py:28
  282.8 15.2 %collective-permute-start.20 = (bf16[256,512]{1,0:T(8,128)(2,1)S(1)}, bf16[256,512]{1,0:T(8,128)(2,1)S(1)}, u32[]{:S(2)}, u32[]{:S(2)}) collective-permute-start(bf16[256,512]{1,0:T(8,128)(2,1)S(1)} %get-tuple-element.32), channel_id=1, source_target_pairs={{0,32},{1,33},{2,34},{3,35},{4,36},{5,37},{6,38},{7,39},{8,160},{9... | collective-permute-start | bytes 786440 | tf_op jit(solution)/shard_map/ppermute | solution.py:28
  (14 other events, 65.5 us)
Sparse Core Ops, SparseCore 0:
  25.0 107.5 all-gather.6
  134.4 55.1 all-gather.8
  191.5 53.4 all-gather.10
where the time goes:
time: 308 us; the launch traced here: 306 us
  waiting for transfers between devices  173 us (56%)
  local copies, waits for them, and re-layouts  41.3 us (13%)
  starting transfers between devices  34.8 us (11%)
  Pallas kernels  24.6 us (8%)
  other arithmetic  16.3 us (5%)
  between operations  14 us (5%)
    ppermute x21, waiting for transfers between devices, permute(): return lax.ppermute(value, AXES, pairs)  144 us
    unnamed x42, local copies, waits for them, and re-layouts  35 us
    ppermute x21, starting transfers between devices, permute(): return lax.ppermute(value, AXES, pairs)  34.7 us
    all_gather x3, waiting for transfers between devices, gather_z(): return lax.all_gather(value, 'fsdp', axis=0, axis_index_groups=groups)  28.6 us
    pallas_call x1, Pallas kernels, project_latents(): pl.pallas_call(latent_kernel, out_shape=(out, out), grid_spec=pltpu.Prefe...  13.8 us
    pallas_call x1, Pallas kernels, project_queries(): pl.pallas_call(query_kernel, out_shape=(out, out), grid_spec=pltpu.Prefet...  7.15 us
  transfers between devices with their start and end apart: 24, of which 15 were waited for; matrix products, arithmetic and copies ran while one was open for 14% of the time, Pallas kernels for 7%

commit v1 on v0

--- a/solution.py
+++ b/solution.py
@@ -52,6 +52,22 @@
     return permute(value, lambda x, yh, c, yl, z: (x, yh ^ (q >> 1), c, yl ^ (q & 1), z))
 
 
+def pick(stacked, index):
+    return lax.dynamic_index_in_dim(stacked, index, 0, keepdims=False)
+
+
+def over_z(value, step):
+    return permute(value, lambda x, yh, c, yl, z: (x, yh, c, yl, (z + step) % NZ))
+
+
+def ring_z(shard):
+    up, down = [shard], [shard]
+    for _ in range(3):
+        up.append(over_z(up[-1], 1))
+        down.append(over_z(down[-1], -1))
+    return down + [over_z(up[-1][:1], 1), over_z(down[-1][1:], -1)] + up[:0:-1]
+
+
 def gather_z(value):
     groups = [list(range(NZ)), list(range(NZ, 2 * NZ))]
     return lax.all_gather(value, "fsdp", axis=0, axis_index_groups=groups)
@@ -61,14 +77,13 @@
     return lax.optimization_barrier((value, *earlier))[0]
 
 
-def gather_y(block):
-    return jnp.stack([block] + [over_y(block, q) for q in (1, 2, 3)])
-
-
-def gather_x(column):
-    up, down = along_x(column, 1), along_x(column, -1)
-    far = [along_x(up[:2], 1), along_x(down[2:], -1)]
-    return jnp.concatenate([column, up, *far, down], axis=0)
+def gather_plane(block):
+    groups = [
+        [((y // 2) * 2 + x * 4 + core) * 16 + (y % 2) * NZ + z for x in range(NX) for y in range(4)]
+        for z in range(NZ)
+        for core in range(NC)
+    ]
+    return lax.all_gather(block, AXES, axis=0, axis_index_groups=groups)
 
 
 def query_kernel(place_ref, own_ref, other_ref, weight_ref, kept, sent):
@@ -85,16 +100,37 @@
     sent[...] += jnp.where(stays, other, own)
 
 
-def latent_kernel(place_ref, mine_ref, theirs_ref, weight_ref, kept, sent):
-    @pl.when(pl.program_id(0) == 0)
+def latent_kernel(place_ref, mine_0, mine_1, theirs_0, theirs_1, *refs):
+    pieces, (kept, sent, held, sems) = refs[:9], refs[9:]
+    k = pl.program_id(0)
+
+    @pl.when(k == 0)
     def _():
-        kept[...] = jnp.zeros_like(kept)
-        sent[...] = jnp.zeros_like(sent)
-
-    for out, latent_ref in ((kept, mine_ref), (sent, theirs_ref)):
-        latent = latent_ref[...]
+        for n, piece in enumerate(pieces):
+            if n in (4, 5):
+                target, sem = held.at[4, pl.ds(n - 4, 1)], sems.at[4]
+            else:
+                target, sem = held.at[n - (n > 5)], sems.at[n - (n > 5)]
+            pltpu.make_async_copy(piece, target, sem).start()
+
+    at = []
+    for j in range(2):
+        d = (weight_at(2 * k + j, place_ref) - place_ref[4] + NZ) % NZ
+        pltpu.make_async_copy(held.at[d], held.at[d], sems.at[d]).wait()
+        at.append(d)
+    for out, low, high in ((kept, mine_0, mine_1), (sent, theirs_0, theirs_1)):
         for n in range(2):
-            out[n] += jnp.dot(latent, weight_ref[n], preferred_element_type=jnp.float32)
+            sums = jnp.dot(low[...], held[at[0], n], preferred_element_type=jnp.float32) + jnp.dot(
+                high[...], held[at[1], n], preferred_element_type=jnp.float32
+            )
+
+            @pl.when(k == 0)
+            def _():
+                out[n] = sums
+
+            @pl.when(k > 0)
+            def _():
+                out[n] += sums
 
 
 def weight_at(s, p):
@@ -102,7 +138,7 @@
 
 
 def project_queries(place, normed, other_half, weights):
-    length = normed.shape[0]
+    length = normed.shape[1]
     steps, depth, width = weights.shape
     out = jax.ShapeDtypeStruct((length, width), jnp.float32)
     whole = pl.BlockSpec((length, width), lambda s, p: (0, 0))
@@ -113,13 +149,13 @@
             num_scalar_prefetch=1,
             grid=(steps,),
             in_specs=[
-                pl.BlockSpec((length, depth), lambda s, p: (0, (s % 2) * 8 + (s // 2) * 2 + p[2])),
+                pl.BlockSpec((None, length, depth), lambda s, p: (p[2], 0, (s % 2) * 4 + s // 2)),
                 pl.BlockSpec((length, depth), lambda s, p: (0, (s % 2) * 4 + s // 2)),
                 pl.BlockSpec((None, depth, width), lambda s, p: (weight_at(s, p), 0, 0)),
             ],
             out_specs=(whole, whole),
         ),
-        compiler_params=pltpu.CompilerParams(vmem_limit_bytes=32 * 2**20),
+        compiler_params=pltpu.CompilerParams(vmem_limit_bytes=56 * 2**20),
         cost_estimate=pl.CostEstimate(
             flops=4 * length * steps * depth * width,
             bytes_accessed=2 * steps * depth * (2 * length + width) + 8 * length * width,
@@ -128,49 +164,50 @@
     )(place, normed, other_half, weights)
 
 
-def project_latents(place, latent_blocks, weights):
+def project_latents(place, latent_blocks, pieces):
     key_count = latent_blocks.shape[1]
-    steps, kinds, depth, width = weights.shape
-
-    def latent_spec(flip):
-        def index(s, p):
-            x_at, y_at = (s % 2) * 2 + s // 4, ((s // 2) % 2) * 2 + (p[2] + flip) % 2
-            return (((p[0] - x_at + NX) % NX) * 4 + (y_at ^ p[1]), 0, 0)
+    kinds, depth, width = pieces[0].shape
+
+    def latent_spec(flip, j):
+        def index(k, p):
+            x_at, y_at = j * 2 + k // 2, (k % 2) * 2 + (p[2] + flip) % 2
+            return (x_at * 4 + y_at, 0, 0)
 
         return pl.BlockSpec((None, key_count, depth), index)
 
     out = jax.ShapeDtypeStruct((kinds, key_count, width), jnp.float32)
-    whole = pl.BlockSpec((kinds, key_count, width), lambda s, p: (0, 0, 0))
+    whole = pl.BlockSpec((kinds, key_count, width), lambda k, p: (0, 0, 0))
     return pl.pallas_call(
         latent_kernel,
         out_shape=(out, out),
         grid_spec=pltpu.PrefetchScalarGridSpec(
             num_scalar_prefetch=1,
-            grid=(steps,),
-            in_specs=[
-                latent_spec(0),
-                latent_spec(1),
-                pl.BlockSpec((None, kinds, depth, width), lambda s, p: (weight_at(s, p), 0, 0, 0)),
+            grid=(NZ // 2,),
+            in_specs=[latent_spec(flip, j) for flip in range(2) for j in range(2)]
+            + [pl.BlockSpec(memory_space=pl.ANY)] * len(pieces),
+            out_specs=(whole, whole),
+            scratch_shapes=[
+                pltpu.VMEM((NZ, kinds, depth, width), jnp.bfloat16),
+                pltpu.SemaphoreType.DMA((NZ,)),
             ],
-            out_specs=(whole, whole),
-        ),
-        compiler_params=pltpu.CompilerParams(vmem_limit_bytes=40 * 2**20),
+        ),
+        compiler_params=pltpu.CompilerParams(vmem_limit_bytes=56 * 2**20),
         cost_estimate=pl.CostEstimate(
-            flops=4 * kinds * key_count * steps * depth * width,
-            bytes_accessed=2 * steps * depth * (2 * key_count + kinds * width)
+            flops=4 * kinds * key_count * NZ * depth * width,
+            bytes_accessed=2 * NZ * depth * (2 * key_count + kinds * width)
             + 8 * kinds * key_count * width,
             transcendentals=0,
         ),
-    )(place, latent_blocks, latent_blocks, weights)
-
-
-def out_kernel(place_ref, mine_ref, theirs_ref, block_ref, *parts):
-    core, y_low, x_high = place_ref[2], place_ref[3], place_ref[0] // 2
+    )(place, *[latent_blocks] * 4, *pieces)
+
+
+def out_kernel(place_ref, mine_ref, theirs_ref, near_ref, far_ref, *parts):
+    core, x_high = place_ref[2], place_ref[0] // 2
 
     def product(ref):
         return (
-            jnp.dot(ref[0], block_ref[y_low], preferred_element_type=jnp.float32)
-            + jnp.dot(ref[1], block_ref[1 - y_low], preferred_element_type=jnp.float32)
+            jnp.dot(ref[0], near_ref[...], preferred_element_type=jnp.float32)
+            + jnp.dot(ref[1], far_ref[...], preferred_element_type=jnp.float32)
         ).astype(jnp.bfloat16)
 
     mine, theirs = product(mine_ref), product(theirs_ref)
@@ -189,8 +226,12 @@
     steps, width = blocks.shape[0] // 2, blocks.shape[2]
     rows = pl.BlockSpec((2, length, depth), lambda s, p: (0, 0, 0))
 
-    def block_index(s, p):
-        return (((s // 2) ^ (p[0] % 2)) * 2 + ((s % 2) ^ (p[1] // 2)), 0, 0)
+    def block_spec(flip):
+        def index(s, p):
+            z = ((s // 2) ^ (p[0] % 2)) * 4 + ((s % 2) ^ (p[1] // 2)) * 2 + (p[3] ^ flip)
+            return (z, 0, 0)
+
+        return pl.BlockSpec((None, depth, width), index)
 
     def out_spec(n):
         def index(s, p):
@@ -204,23 +245,47 @@
         grid_spec=pltpu.PrefetchScalarGridSpec(
             num_scalar_prefetch=1,
             grid=(steps,),
-            in_specs=[rows, rows, pl.BlockSpec((2, depth, width), block_index)],
+            in_specs=[rows, rows, block_spec(0), block_spec(1)],
             out_specs=[out_spec(n % 2) for n in range(4)],
         ),
-        compiler_params=pltpu.CompilerParams(vmem_limit_bytes=32 * 2**20),
+        compiler_params=pltpu.CompilerParams(vmem_limit_bytes=56 * 2**20),
         cost_estimate=pl.CostEstimate(
             flops=8 * length * depth * steps * width,
             bytes_accessed=2 * (4 * length * depth + 2 * steps * depth * width + 8 * length * width),
             transcendentals=0,
         ),
-    )(place, mine, theirs, blocks)
-
-
-def layer_norm(text_rows, norm_gain):
-    values = text_rows.astype(jnp.float32)
+    )(place, mine, theirs, blocks, blocks)
+
+
+def norm_kernel(text_ref, gain_ref, out_ref):
+    values = text_ref[...].astype(jnp.float32)
     center = jnp.mean(values, axis=-1, keepdims=True)
     spread = jnp.mean(jnp.square(values - center), axis=-1, keepdims=True)
-    return ((values - center) * lax.rsqrt(spread + 1e-05) * norm_gain).astype(jnp.bfloat16)
+    normed = ((values - center) * lax.rsqrt(spread + 1e-05) * gain_ref[...]).astype(jnp.bfloat16)
+    width = out_ref.shape[2] // NZ
+    for n in range(2 * NZ):
+        out_ref[n % 2, :, n // 2 * width : (n // 2 + 1) * width] = normed[:, n * width : (n + 1) * width]
+
+
+def layer_norm(text_rows, norm_gain):
+    length, model_width = text_rows.shape
+    rows = 32
+    return pl.pallas_call(
+        norm_kernel,
+        out_shape=jax.ShapeDtypeStruct((2, length, model_width // 2), jnp.bfloat16),
+        grid=(length // rows,),
+        in_specs=[
+            pl.BlockSpec((rows, model_width), lambda s: (s, 0)),
+            pl.BlockSpec((1, model_width), lambda s: (0, 0)),
+        ],
+        out_specs=pl.BlockSpec((2, rows, model_width // 2), lambda s: (0, s, 0)),
+        compiler_params=pltpu.CompilerParams(vmem_limit_bytes=32 * 2**20),
+        cost_estimate=pl.CostEstimate(
+            flops=8 * length * model_width,
+            bytes_accessed=4 * length * model_width,
+            transcendentals=length,
+        ),
+    )(text_rows, norm_gain[None])
 
 
 def attention_weights(queries, keys, token_image):
@@ -267,23 +332,18 @@
     width = w_out.shape[1]
     section, place = lax.axis_index("section"), lax.axis_index("fsdp")
     x, yh, core, yl = section // 4, (section // 2) % 2, section % 2, place // NZ
-    here = jnp.stack([x, yh * 2 + yl, core, yl]).astype(jnp.int32)
-
-    latent_shard = to_parity(jnp.stack([w_key, w_value]))
-    latent_weights = gather_z(latent_shard)
-    column = gather_y(latents[0])
-    latent_blocks = gather_x(column)
-    query_shard = to_parity(after(w_query, column, latent_shard))
-    query_weights = gather_z(query_shard)
+    here = jnp.stack([x, yh * 2 + yl, core, yl, place % NZ]).astype(jnp.int32)
+
+    latent_blocks = gather_plane(latents[0])
+    latent_weights = ring_z(to_parity(jnp.stack([w_key, w_value])))
+    one_away, two_away = (latent_weights[1], latent_weights[8]), (latent_weights[2], latent_weights[7])
+    query_weights = gather_z(to_parity(after(w_query, *one_away)))
+    out_weights = gather_z(swap_core_parity(after(w_out, *two_away)))
 
     normed = layer_norm(text_states[0], norm_gain)
-    own_half = jnp.concatenate(
-        [lax.dynamic_slice_in_dim(normed, (2 * n + core) * width, width, 1) for n in range(NZ)], axis=1
-    )
-    other_half = over_y(after(own_half, query_shard), 1)
-    out_shard = swap_core_parity(after(w_out, query_shard))
-    out_blocks = gather_z(out_shard)
-    other_image = over_y(after(token_image, out_shard), 1)
+    own_half = pick(normed, core)
+    other_half = over_y(after(own_half, *one_away), 1)
+    other_image = over_y(after(token_image, *two_away), 1)
     images = jnp.where(core == yl, token_image, other_image)[0]
 
     kept, sent = project_queries(here, normed, other_half, query_weights)
@@ -293,7 +353,7 @@
     attended = attend(attention_weights(queries, keys, images), values)
 
     mine = jnp.stack([attended, over_y(attended, 1)])
-    parts = partial_sums(here, mine, swap_cores(mine), out_blocks)
+    parts = partial_sums(here, mine, swap_cores(mine), out_weights)
     near = total(parts[0], [over_x(parts[r], r) for r in (1, 2, 3)]).astype(jnp.bfloat16)
     projected = total(to_final(near[0], 0), [to_final(near[1], 1)])
     own_text = lax.dynamic_slice_in_dim(text_states[0], section * width, width, 1)

time: 308 us -> 293 us (0.951)
  local copies, waits for them, and re-layouts: 41.3 us -> 8.78 us
  starting transfers between devices: 34.8 us -> 61.6 us
  Pallas kernels: 24.6 us -> 39.9 us
  waiting for transfers between devices: 173 us -> 160 us
  other arithmetic: 16.3 us -> 6.22 us
    unnamed x42 -> x28, local copies, waits for them, and re-layouts: 35 us -> 3.92 us
    ppermute x21 -> x22, starting transfers between devices: 34.7 us -> 61.6 us  [permute(): return lax.ppermute(value, AXES, pairs)]
    all_gather x3 -> x2, waiting for transfers between devices: 28.6 us -> 6.38 us  [gather_z(): return lax.all_gather(value, 'fsdp', axis=0, axis_index_groups=groups)]
    ppermute x21 -> x22, waiting for transfers between devices: 144 us -> 153 us  [permute(): return lax.ppermute(value, AXES, pairs)]
    pallas_call x1, Pallas kernels: 13.8 us -> 19.1 us  [project_latents(): pl.pallas_call(latent_kernel, out_shape=(out, out), grid_spec=pltpu.Prefe...]
    pallas_call x0 -> x1, Pallas kernels: none -> 4.44 us  [layer_norm(): pl.pallas_call(norm_kernel, out_shape=jax.ShapeDtypeStruct((2, length, mo...]
    reduce_sum x2 -> x0, other arithmetic: 4.28 us -> none  [the longest x1 3.04 us: layer_norm(): center = jnp.mean(values, axis=-1, keepdims=True)]
    convert_element_type x1 -> x0, other arithmetic: 3.73 us -> none  [layer_norm(): ((values - center) * lax.rsqrt(spread + 1e-05) * norm_gain).astype(jnp.bf...]
  transfers between devices with their start and end apart: 24 -> 25, of which waited for: 15 -> 17; matrix products, arithmetic and copies ran while one was open for 14% -> 3% of each run, Pallas kernels for 7% -> 11%
where the time goes in v1:
time: 293 us; the launch traced here: 292 us
  waiting for transfers between devices  160 us (55%)
  starting transfers between devices  61.6 us (21%)
  Pallas kernels  39.9 us (14%)
  between operations  14 us (5%)
  local copies, waits for them, and re-layouts  8.78 us (3%)
  other arithmetic  6.22 us (2%)
    ppermute x22, waiting for transfers between devices, permute(): return lax.ppermute(value, AXES, pairs)  153 us
    ppermute x22, starting transfers between devices, permute(): return lax.ppermute(value, AXES, pairs)  61.6 us
    pallas_call x1, Pallas kernels, project_latents(): pl.pallas_call(latent_kernel, out_shape=(out, out), grid_spec=pltpu.Prefe...  19.1 us
    pallas_call x1, Pallas kernels, project_queries(): pl.pallas_call(query_kernel, out_shape=(out, out), grid_spec=pltpu.Prefet...  9.43 us
    pallas_call x1, Pallas kernels, partial_sums(): pl.pallas_call(out_kernel, out_shape=[jax.ShapeDtypeStruct((2, length, wi...  6.99 us
    all_gather x2, waiting for transfers between devices, gather_z(): return lax.all_gather(value, 'fsdp', axis=0, axis_index_groups=groups)  6.38 us
  transfers between devices with their start and end apart: 25, of which 17 were waited for; matrix products, arithmetic and copies ran while one was open for 3% of the time, Pallas kernels for 11%

profile of v1, /device:TPU:8, one launch (start us, length us, event | category | flops | bytes accessed | tf_op | source)
XLA Modules:
  0.0 291.9 jit_solution(5428879390524557780)
XLA Ops:
  8.7 3.7 %collective-permute-start = (bf16[2,512,512]{2,1,0:T(8,128)(2,1)S(1)}, bf16[2,512,512]{2,1,0:T(8,128)(2,1)S(1)}, u32[]{:S(2)}, u32[]{:S(2)}) collective-permute-start(bf16[2,512,512]{2,1,0:T(8,128)(2,1)S(1)} %pad_maximum_fusion), channel_id=1, source_target_pairs={{0,0},{1,17},{2,2},{3,19},{4,4},{5,21},{6,6},{7,23},{8,1},{9,16},{... | collective-permute-start | bytes 3145736 | tf_op jit(solution)/shard_map/ppermute | solution.py:28
  12.4 12.3 %collective-permute-done.refs_0_ = bf16[2,512,512]{2,1,0:T(8,128)(2,1)S(1)} collective-permute-done((bf16[2,512,512]{2,1,0:T(8,128)(2,1)S(1)}, bf16[2,512,512]{2,1,0:T(8,128)(2,1)S(1)}, u32[]{:S(2)}, u32[]{:S(2)}) %collective-permute-start) | collective-permute-done | bytes 1048608 | tf_op jit(solution)/shard_map/ppermute | solution.py:28
  24.7 7.0 %collective-permute-start.1 = (bf16[2,512,512]{2,1,0:T(8,128)(2,1)S(1)}, bf16[2,512,512]{2,1,0:T(8,128)(2,1)S(1)}, u32[]{:S(2)}, u32[]{:S(2)}) collective-permute-start(bf16[2,512,512]{2,1,0:T(8,128)(2,1)S(1)} %collective-permute-done.refs_0_), channel_id=1, source_target_pairs={{0,7},{1,0},{2,1},{3,2},{4,3},{5,4},{6,5},{7,6},{8,15},{9,8},{10,9... | collective-permute-start | bytes 3145736 | tf_op jit(solution)/shard_map/ppermute | solution.py:28
  31.7 18.4 %collective-permute-done.1.refs_1_ = bf16[2,512,512]{2,1,0:T(8,128)(2,1)S(1)} collective-permute-done((bf16[2,512,512]{2,1,0:T(8,128)(2,1)S(1)}, bf16[2,512,512]{2,1,0:T(8,128)(2,1)S(1)}, u32[]{:S(2)}, u32[]{:S(2)}) %collective-permute-start.1) | collective-permute-done | bytes 1048608 | tf_op jit(solution)/shard_map/ppermute | solution.py:28
  50.0 4.8 %collective-permute-done.4.refs_8_ = bf16[2,512,512]{2,1,0:T(8,128)(2,1)S(1)} collective-permute-done((bf16[2,512,512]{2,1,0:T(8,128)(2,1)S(1)}, bf16[2,512,512]{2,1,0:T(8,128)(2,1)S(1)}, u32[]{:S(2)}, u32[]{:S(2)}) %collective-permute-start.4) | collective-permute-done | bytes 1048608 | tf_op jit(solution)/shard_map/ppermute | solution.py:28
  56.8 6.7 %collective-permute-done.12 = bf16[512,512]{1,0:T(8,128)(2,1)} collective-permute-done((bf16[512,512]{1,0:T(8,128)(2,1)S(1)}, bf16[512,512]{1,0:T(8,128)(2,1)}, u32[]{:S(2)}, u32[]{:S(2)}) %collective-permute-start.12) | collective-permute-done | bytes 524320 | tf_op jit(solution)/shard_map/ppermute | solution.py:28
  63.6 4.8 %collective-permute-start.2 = (bf16[2,512,512]{2,1,0:T(8,128)(2,1)S(1)}, bf16[2,512,512]{2,1,0:T(8,128)(2,1)}, u32[]{:S(2)}, u32[]{:S(2)}) collective-permute-start(bf16[2,512,512]{2,1,0:T(8,128)(2,1)S(1)} %collective-permute-done.1.refs_1_), channel_id=1, source_target_pairs={{0,7},{1,0},{2,1},{3,2},{4,3},{5,4},{6,5},{7,6},{8,15},{9,8},{10,9... | collective-permute-start | bytes 3145736 | tf_op jit(solution)/shard_map/ppermute | solution.py:28
  68.4 19.1 %collective-permute-done.2.refs_2_ = bf16[2,512,512]{2,1,0:T(8,128)(2,1)} collective-permute-done((bf16[2,512,512]{2,1,0:T(8,128)(2,1)S(1)}, bf16[2,512,512]{2,1,0:T(8,128)(2,1)}, u32[]{:S(2)}, u32[]{:S(2)}) %collective-permute-start.2) | collective-permute-done | bytes 1048608 | tf_op jit(solution)/shard_map/ppermute | solution.py:28
  90.8 5.4 %collective-permute-start.16 = (bf16[512,512]{1,0:T(8,128)(2,1)}, bf16[512,512]{1,0:T(8,128)(2,1)}, u32[]{:S(2)}, u32[]{:S(2)}) collective-permute-start(bf16[512,512]{1,0:T(8,128)(2,1)} %param.15), channel_id=1, source_target_pairs={{0,0},{1,16},{2,2},{3,18},{4,4},{5,20},{6,6},{7,22},{8,8},{9,24},{... | collective-permute-start | bytes 1572872 | tf_op jit(solution)/shard_map/ppermute | solution.py:28
  99.5 33.7 %collective-permute-done.6.refs_6_ = bf16[2,512,512]{2,1,0:T(8,128)(2,1)S(1)} collective-permute-done((bf16[2,512,512]{2,1,0:T(8,128)(2,1)}, bf16[2,512,512]{2,1,0:T(8,128)(2,1)S(1)}, u32[]{:S(2)}, u32[]{:S(2)}) %collective-permute-start.6) | collective-permute-done | bytes 1048608 | tf_op jit(solution)/shard_map/ppermute | solution.py:28
  137.3 4.4 %collective-permute-start.8 = (bf16[1,512,512]{2,1,0:T(8,128)(2,1)}, bf16[1,512,512]{2,1,0:T(8,128)(2,1)}, u32[]{:S(2)}, u32[]{:S(2)}) collective-permute-start(bf16[1,512,512]{2,1,0:T(8,128)(2,1)} %slice.17), channel_id=1, source_target_pairs={{0,7},{1,0},{2,1},{3,2},{4,3},{5,4},{6,5},{7,6},{8,15},{9,8},{10,9... | collective-permute-start | bytes 1572872 | tf_op jit(solution)/shard_map/ppermute | solution.py:28
  144.6 4.4 %shard_map.92.own_ref = bf16[2,256,4096]{2,1,0:T(8,128)(2,1)S(1)} custom-call(bf16[256,8192]{1,0:T(8,128)(2,1)S(1)} %bitcast.41, f32[1,8192]{1,0:T(1,128)S(1)} %bitcast.42), custom_call_target="tpu_custom_call" | custom-call | flops 16777216 | bytes 8388608 | tf_op jit(solution)/shard_map/pallas_call | solution.py:273
  154.6 5.3 %collective-permute-done.7.refs_4_ = bf16[1,512,512]{2,1,0:T(8,128)(2,1)} collective-permute-done((bf16[1,512,512]{2,1,0:T(8,128)(2,1)}, bf16[1,512,512]{2,1,0:T(8,128)(2,1)}, u32[]{:S(2)}, u32[]{:S(2)}) %collective-permute-start.7) | collective-permute-done | bytes 524320 | tf_op jit(solution)/shard_map/ppermute | solution.py:28
  161.8 19.1 %shard_map.91 = (f32[2,512,512]{2,1,0:T(8,128)}, f32[2,512,512]{2,1,0:T(8,128)}) custom-call(s32[5]{0:T(128)} %stack.38.place_ref, bf16[16,512,512]{2,1,0:T(8,128)(2,1)} %all-gather.6.cloned.1.call-done.mine_0.mine_1.theirs_0.theirs_1, bf16[16,512,512]{2,1,0:T(8,128)(2,1)} %all-gather.6.cloned.1.call-done.mine_0.mine_1.theirs_0.theirs_1, ...), custom_call_target="tpu_custom_call" | custom-call | flops 8589934592 | bytes 20971520 | tf_op jit(solution)/shard_map/pallas_call | solution.py:180
  180.8 5.7 %collective-permute-start.9 = (f32[2,512,512]{2,1,0:T(8,128)}, f32[2,512,512]{2,1,0:T(8,128)S(1)}, u32[]{:S(2)}, u32[]{:S(2)}) collective-permute-start(f32[2,512,512]{2,1,0:T(8,128)} %get-tuple-element.18), channel_id=1, source_target_pairs={{0,16},{1,17},{2,18},{3,19},{4,20},{5,21},{6,22},{7,23},{8,24},{9,... | collective-permute-start | bytes 6291464 | tf_op jit(solution)/shard_map/ppermute | solution.py:28
  188.7 8.9 %collective-permute-done.10 = s32[1,256]{1,0:T(1,128)S(1)} collective-permute-done((s32[1,256]{1,0:T(1,128)S(1)}, s32[1,256]{1,0:T(1,128)S(1)}, u32[]{:S(2)}, u32[]{:S(2)}) %collective-permute-start.10) | collective-permute-done | bytes 1056 | tf_op jit(solution)/shard_map/ppermute | solution.py:28
  198.0 9.4 %shard_map.93 = (f32[256,512]{1,0:T(8,128)}, f32[256,512]{1,0:T(8,128)}) custom-call(s32[5]{0:T(128)} %stack.38.place_ref, bf16[2,256,4096]{2,1,0:T(8,128)(2,1)} %copy-done, bf16[256,4096]{1,0:T(8,128)(2,1)} %collective-permute-done.11.other_ref, bf16[8,512,512]{2,1,0:T(8,128)(2,1)} %bitcast.45), custom_call_target="tpu_custom_call" | custom-call | flops 2147483648 | bytes 9437184 | tf_op jit(solution)/shard_map/pallas_call | solution.py:145
  207.5 3.9 %collective-permute-start.13 = (f32[256,512]{1,0:T(8,128)}, f32[256,512]{1,0:T(8,128)S(1)}, u32[]{:S(2)}, u32[]{:S(2)}) collective-permute-start(f32[256,512]{1,0:T(8,128)} %get-tuple-element.23), channel_id=1, source_target_pairs={{0,16},{1,17},{2,18},{3,19},{4,20},{5,21},{6,22},{7,23},{8,24},{9,... | collective-permute-start | bytes 1572872 | tf_op jit(solution)/shard_map/ppermute | solution.py:28
  218.0 6.7 %collective-permute-done.14 = bf16[256,512]{1,0:T(8,128)(2,1)S(1)} collective-permute-done((bf16[256,512]{1,0:T(8,128)(2,1)S(1)}, bf16[256,512]{1,0:T(8,128)(2,1)S(1)}, u32[]{:S(2)}, u32[]{:S(2)}) %collective-permute-start.14) | collective-permute-done | bytes 262176 | tf_op jit(solution)/shard_map/ppermute | solution.py:28
  224.8 6.4 %all-gather.10.cloned.1.call-done = bf16[4096,512]{1,0:T(8,128)(2,1)} async-done(((bf16[512,512]{1,0:T(8,128)(2,1)}), bf16[4096,512]{1,0:T(8,128)(2,1)}) %all-gather.10.cloned.1.call-update) | async-done | bytes 4194320 | tf_op jit(solution)/shard_map/all_gather | solution.py:73
  232.0 7.0 %shard_map.94 = (bf16[2,256,512]{2,1,0:T(8,128)(2,1)}, bf16[2,256,512]{2,1,0:T(8,128)(2,1)}, bf16[2,256,512]{2,1,0:T(8,128)(2,1)}, bf16[2,256,512]{2,1,0:T(8,128)(2,1)}) custom-call(s32[5]{0:T(128)} %stack.38.place_ref, bf16[2,256,512]{2,1,0:T(8,128)(2,1)} %copy-done.5, bf16[2,256,512]{2,1,0:T(8,128)(2,1)} %copy-done.10, bf16[8,512,512]{2,1,0:T(8,128)(2,1)} %bitcast.43, ...), custom_call_target="tpu_custom_call" | custom-call | flops 2147483648 | bytes 7340032 | tf_op jit(solution)/shard_map/pallas_call | solution.py:242
  243.1 22.2 %collective-permute-done.19 = bf16[2,256,512]{2,1,0:T(8,128)(2,1)S(1)} collective-permute-done((bf16[2,256,512]{2,1,0:T(8,128)(2,1)}, bf16[2,256,512]{2,1,0:T(8,128)(2,1)S(1)}, u32[]{:S(2)}, u32[]{:S(2)}) %collective-permute-start.19) | collective-permute-done | bytes 524320 | tf_op jit(solution)/shard_map/ppermute | solution.py:28
  267.3 4.0 %collective-permute-start.21 = (bf16[256,512]{1,0:T(8,128)(2,1)S(1)}, bf16[256,512]{1,0:T(8,128)(2,1)S(1)}, u32[]{:S(2)}, u32[]{:S(2)}) collective-permute-start(bf16[256,512]{1,0:T(8,128)(2,1)S(1)} %get-tuple-element.32), channel_id=1, source_target_pairs={{0,32},{1,33},{2,34},{3,35},{4,36},{5,37},{6,38},{7,39},{8,160},{9... | collective-permute-start | bytes 786440 | tf_op jit(solution)/shard_map/ppermute | solution.py:28
  277.9 5.7 %collective-permute-done.20 = bf16[256,512]{1,0:T(8,128)(2,1)S(1)} collective-permute-done((bf16[256,512]{1,0:T(8,128)(2,1)S(1)}, bf16[256,512]{1,0:T(8,128)(2,1)S(1)}, u32[]{:S(2)}, u32[]{:S(2)}) %collective-permute-start.20) | collective-permute-done | bytes 262176 | tf_op jit(solution)/shard_map/ppermute | solution.py:28
  (85 shorter events, 48.9 us)
Async XLA Ops:
  6.5 155.2 %all-gather.6.cloned.1.call-start = ((), (), s32[]{:S(2)}) async-start(), calls=%async_computation | async-start | bytes 8912896 | tf_op jit(solution)/shard_map/all_gather | solution.py:86
  7.3 190.8 %all-gather.8.cloned.1.call-start = ((), (), s32[]{:S(2)}) async-start(), calls=%async_computation.1 | async-start | bytes 4718592 | tf_op jit(solution)/shard_map/all_gather | solution.py:73
  8.7 16.0 %collective-permute-start = (bf16[2,512,512]{2,1,0:T(8,128)(2,1)S(1)}, bf16[2,512,512]{2,1,0:T(8,128)(2,1)S(1)}, u32[]{:S(2)}, u32[]{:S(2)}) collective-permute-start(bf16[2,512,512]{2,1,0:T(8,128)(2,1)S(1)} %pad_maximum_fusion), channel_id=1, source_target_pairs={{0,0},{1,17},{2,2},{3,19},{4,4},{5,21},{6,6},{7,23},{8,1},{9,16},{... | collective-permute-start | bytes 3145736 | tf_op jit(solution)/shard_map/ppermute | solution.py:28
  24.7 25.3 %collective-permute-start.1 = (bf16[2,512,512]{2,1,0:T(8,128)(2,1)S(1)}, bf16[2,512,512]{2,1,0:T(8,128)(2,1)S(1)}, u32[]{:S(2)}, u32[]{:S(2)}) collective-permute-start(bf16[2,512,512]{2,1,0:T(8,128)(2,1)S(1)} %collective-permute-done.refs_0_), channel_id=1, source_target_pairs={{0,7},{1,0},{2,1},{3,2},{4,3},{5,4},{6,5},{7,6},{8,15},{9,8},{10,9... | collective-permute-start | bytes 3145736 | tf_op jit(solution)/shard_map/ppermute | solution.py:28
  31.7 23.2 %collective-permute-start.4 = (bf16[2,512,512]{2,1,0:T(8,128)(2,1)S(1)}, bf16[2,512,512]{2,1,0:T(8,128)(2,1)S(1)}, u32[]{:S(2)}, u32[]{:S(2)}) collective-permute-start(bf16[2,512,512]{2,1,0:T(8,128)(2,1)S(1)} %collective-permute-done.refs_0_), channel_id=1, source_target_pairs={{0,1},{1,2},{2,3},{3,4},{4,5},{5,6},{6,7},{7,0},{8,9},{9,10},{10,1... | collective-permute-start | bytes 3145736 | tf_op jit(solution)/shard_map/ppermute | solution.py:28
  54.9 8.6 %collective-permute-start.12 = (bf16[512,512]{1,0:T(8,128)(2,1)S(1)}, bf16[512,512]{1,0:T(8,128)(2,1)}, u32[]{:S(2)}, u32[]{:S(2)}) collective-permute-start(bf16[512,512]{1,0:T(8,128)(2,1)S(1)} %copy-done.13), channel_id=1, source_target_pairs={{0,0},{1,17},{2,2},{3,19},{4,4},{5,21},{6,6},{7,23},{8,1},{9,16},{... | collective-permute-start | bytes 1572872 | tf_op jit(solution)/shard_map/ppermute | solution.py:28
  63.5 167.6 %all-gather.10.cloned.1.call-start = ((), (), s32[]{:S(2)}) async-start(), calls=%async_computation.2 | async-start | bytes 4718592 | tf_op jit(solution)/shard_map/all_gather | solution.py:73
  63.6 23.9 %collective-permute-start.2 = (bf16[2,512,512]{2,1,0:T(8,128)(2,1)S(1)}, bf16[2,512,512]{2,1,0:T(8,128)(2,1)}, u32[]{:S(2)}, u32[]{:S(2)}) collective-permute-start(bf16[2,512,512]{2,1,0:T(8,128)(2,1)S(1)} %collective-permute-done.1.refs_1_), channel_id=1, source_target_pairs={{0,7},{1,0},{2,1},{3,2},{4,3},{5,4},{6,5},{7,6},{8,15},{9,8},{10,9... | collective-permute-start | bytes 3145736 | tf_op jit(solution)/shard_map/ppermute | solution.py:28
  68.4 22.5 %collective-permute-start.5 = (bf16[2,512,512]{2,1,0:T(8,128)(2,1)S(1)}, bf16[2,512,512]{2,1,0:T(8,128)(2,1)}, u32[]{:S(2)}, u32[]{:S(2)}) collective-permute-start(bf16[2,512,512]{2,1,0:T(8,128)(2,1)S(1)} %collective-permute-done.4.refs_8_), channel_id=1, source_target_pairs={{0,1},{1,2},{2,3},{3,4},{4,5},{5,6},{6,7},{7,0},{8,9},{9,10},{10,1... | collective-permute-start | bytes 3145736 | tf_op jit(solution)/shard_map/ppermute | solution.py:28
  90.8 8.6 %collective-permute-start.16 = (bf16[512,512]{1,0:T(8,128)(2,1)}, bf16[512,512]{1,0:T(8,128)(2,1)}, u32[]{:S(2)}, u32[]{:S(2)}) collective-permute-start(bf16[512,512]{1,0:T(8,128)(2,1)} %param.15), channel_id=1, source_target_pairs={{0,0},{1,16},{2,2},{3,18},{4,4},{5,20},{6,6},{7,22},{8,8},{9,24},{... | collective-permute-start | bytes 1572872 | tf_op jit(solution)/shard_map/ppermute | solution.py:28
  96.2 37.0 %collective-permute-start.6 = (bf16[2,512,512]{2,1,0:T(8,128)(2,1)}, bf16[2,512,512]{2,1,0:T(8,128)(2,1)S(1)}, u32[]{:S(2)}, u32[]{:S(2)}) collective-permute-start(bf16[2,512,512]{2,1,0:T(8,128)(2,1)} %collective-permute-done.5.refs_7_), channel_id=1, source_target_pairs={{0,1},{1,2},{2,3},{3,4},{4,5},{5,6},{6,7},{7,0},{8,9},{9,10},{10,1... | collective-permute-start | bytes 3145736 | tf_op jit(solution)/shard_map/ppermute | solution.py:28
  96.2 40.3 %collective-permute-start.3 = (bf16[2,512,512]{2,1,0:T(8,128)(2,1)}, bf16[2,512,512]{2,1,0:T(8,128)(2,1)S(1)}, u32[]{:S(2)}, u32[]{:S(2)}) collective-permute-start(bf16[2,512,512]{2,1,0:T(8,128)(2,1)} %collective-permute-done.2.refs_2_), channel_id=1, source_target_pairs={{0,7},{1,0},{2,1},{3,2},{4,3},{5,4},{6,5},{7,6},{8,15},{9,8},{10,9... | collective-permute-start | bytes 3145736 | tf_op jit(solution)/shard_map/ppermute | solution.py:28
  134.1 25.8 %collective-permute-start.7 = (bf16[1,512,512]{2,1,0:T(8,128)(2,1)}, bf16[1,512,512]{2,1,0:T(8,128)(2,1)}, u32[]{:S(2)}, u32[]{:S(2)}) collective-permute-start(bf16[1,512,512]{2,1,0:T(8,128)(2,1)} %slice.16), channel_id=1, source_target_pairs={{0,1},{1,2},{2,3},{3,4},{4,5},{5,6},{6,7},{7,0},{8,9},{9,10},{10,1... | collective-permute-start | bytes 1572872 | tf_op jit(solution)/shard_map/ppermute | solution.py:28
  137.3 24.4 %collective-permute-start.8 = (bf16[1,512,512]{2,1,0:T(8,128)(2,1)}, bf16[1,512,512]{2,1,0:T(8,128)(2,1)}, u32[]{:S(2)}, u32[]{:S(2)}) collective-permute-start(bf16[1,512,512]{2,1,0:T(8,128)(2,1)} %slice.17), channel_id=1, source_target_pairs={{0,7},{1,0},{2,1},{3,2},{4,3},{5,4},{6,5},{7,6},{8,15},{9,8},{10,9... | collective-permute-start | bytes 1572872 | tf_op jit(solution)/shard_map/ppermute | solution.py:28
  151.7 46.3 %collective-permute-start.11 = (bf16[256,4096]{1,0:T(8,128)(2,1)}, bf16[256,4096]{1,0:T(8,128)(2,1)}, u32[]{:S(2)}, u32[]{:S(2)}) collective-permute-start(bf16[256,4096]{1,0:T(8,128)(2,1)} %dynamic-slice_bitcast_fusion), channel_id=1, source_target_pairs={{0,8},{1,9},{2,10},{3,11},{4,12},{5,13},{6,14},{7,15},{8,0},{9,1},... | collective-permute-start | bytes 6291464 | tf_op jit(solution)/shard_map/ppermute | solution.py:28
  180.8 30.6 %collective-permute-start.9 = (f32[2,512,512]{2,1,0:T(8,128)}, f32[2,512,512]{2,1,0:T(8,128)S(1)}, u32[]{:S(2)}, u32[]{:S(2)}) collective-permute-start(f32[2,512,512]{2,1,0:T(8,128)} %get-tuple-element.18), channel_id=1, source_target_pairs={{0,16},{1,17},{2,18},{3,19},{4,20},{5,21},{6,22},{7,23},{8,24},{9,... | collective-permute-start | bytes 6291464 | tf_op jit(solution)/shard_map/ppermute | solution.py:28
  186.5 11.1 %collective-permute-start.10 = (s32[1,256]{1,0:T(1,128)S(1)}, s32[1,256]{1,0:T(1,128)S(1)}, u32[]{:S(2)}, u32[]{:S(2)}) collective-permute-start(s32[1,256]{1,0:T(1,128)S(1)} %copy-done.12), channel_id=1, source_target_pairs={{0,8},{1,9},{2,10},{3,11},{4,12},{5,13},{6,14},{7,15},{8,0},{9,1},... | collective-permute-start | bytes 3080 | tf_op jit(solution)/shard_map/ppermute | solution.py:28
  215.7 8.9 %collective-permute-start.14 = (bf16[256,512]{1,0:T(8,128)(2,1)S(1)}, bf16[256,512]{1,0:T(8,128)(2,1)S(1)}, u32[]{:S(2)}, u32[]{:S(2)}) collective-permute-start(bf16[256,512]{1,0:T(8,128)(2,1)S(1)} %copy.27), channel_id=1, source_target_pairs={{0,8},{1,9},{2,10},{3,11},{4,12},{5,13},{6,14},{7,15},{8,0},{9,1},... | collective-permute-start | bytes 786440 | tf_op jit(solution)/shard_map/ppermute | solution.py:28
  224.7 6.5 %collective-permute-start.15 = (bf16[2,256,512]{2,1,0:T(8,128)(2,1)S(1)}, bf16[2,256,512]{2,1,0:T(8,128)(2,1)S(1)}, u32[]{:S(2)}, u32[]{:S(2)}) collective-permute-start(bf16[2,256,512]{2,1,0:T(8,128)(2,1)S(1)} %pad_maximum_fusion.1.mine_ref), channel_id=1, source_target_pairs={{0,16},{1,17},{2,18},{3,19},{4,20},{5,21},{6,22},{7,23},{8,24},{9,... | collective-permute-start | bytes 1572872 | tf_op jit(solution)/shard_map/ppermute | solution.py:28
  239.0 26.3 %collective-permute-start.19 = (bf16[2,256,512]{2,1,0:T(8,128)(2,1)}, bf16[2,256,512]{2,1,0:T(8,128)(2,1)S(1)}, u32[]{:S(2)}, u32[]{:S(2)}) collective-permute-start(bf16[2,256,512]{2,1,0:T(8,128)(2,1)} %get-tuple-element.28), channel_id=1, source_target_pairs={{0,192},{1,193},{2,194},{3,195},{4,196},{5,197},{6,198},{7,199},{8... | collective-permute-start | bytes 1572872 | tf_op jit(solution)/shard_map/ppermute | solution.py:28
  241.7 23.6 %collective-permute-start.18 = (bf16[2,256,512]{2,1,0:T(8,128)(2,1)}, bf16[2,256,512]{2,1,0:T(8,128)(2,1)S(1)}, u32[]{:S(2)}, u32[]{:S(2)}) collective-permute-start(bf16[2,256,512]{2,1,0:T(8,128)(2,1)} %get-tuple-element.27), channel_id=1, source_target_pairs={{0,128},{1,129},{2,130},{3,131},{4,132},{5,133},{6,134},{7,135},{8... | collective-permute-start | bytes 1572872 | tf_op jit(solution)/shard_map/ppermute | solution.py:28
  242.5 23.4 %collective-permute-start.17 = (bf16[2,256,512]{2,1,0:T(8,128)(2,1)}, bf16[2,256,512]{2,1,0:T(8,128)(2,1)S(1)}, u32[]{:S(2)}, u32[]{:S(2)}) collective-permute-start(bf16[2,256,512]{2,1,0:T(8,128)(2,1)} %get-tuple-element.26), channel_id=1, source_target_pairs={{0,64},{1,65},{2,66},{3,67},{4,68},{5,69},{6,70},{7,71},{8,72},{9,... | collective-permute-start | bytes 1572872 | tf_op jit(solution)/shard_map/ppermute | solution.py:28
  267.3 10.6 %collective-permute-start.21 = (bf16[256,512]{1,0:T(8,128)(2,1)S(1)}, bf16[256,512]{1,0:T(8,128)(2,1)S(1)}, u32[]{:S(2)}, u32[]{:S(2)}) collective-permute-start(bf16[256,512]{1,0:T(8,128)(2,1)S(1)} %get-tuple-element.32), channel_id=1, source_target_pairs={{0,32},{1,33},{2,34},{3,35},{4,36},{5,37},{6,38},{7,39},{8,160},{9... | collective-permute-start | bytes 786440 | tf_op jit(solution)/shard_map/ppermute | solution.py:28
  271.3 12.3 %collective-permute-start.20 = (bf16[256,512]{1,0:T(8,128)(2,1)S(1)}, bf16[256,512]{1,0:T(8,128)(2,1)S(1)}, u32[]{:S(2)}, u32[]{:S(2)}) collective-permute-start(bf16[256,512]{1,0:T(8,128)(2,1)S(1)} %get-tuple-element.31), channel_id=1, source_target_pairs={{0,0},{1,1},{2,2},{3,3},{4,4},{5,5},{6,6},{7,7},{8,128},{9,129},{1... | collective-permute-start | bytes 786440 | tf_op jit(solution)/shard_map/ppermute | solution.py:28
  (15 other events, 483.4 us)
Sparse Core Ops, SparseCore 0:
  9.8 81.8 all-gather.5
  93.4 80.5 all-gather.7
  175.8 55.2 all-gather.9

commit v2 on v1

--- a/solution.py
+++ b/solution.py
@@ -155,7 +155,7 @@
             ],
             out_specs=(whole, whole),
         ),
-        compiler_params=pltpu.CompilerParams(vmem_limit_bytes=56 * 2**20),
+        compiler_params=pltpu.CompilerParams(vmem_limit_bytes=16 * 2**20),
         cost_estimate=pl.CostEstimate(
             flops=4 * length * steps * depth * width,
             bytes_accessed=2 * steps * depth * (2 * length + width) + 8 * length * width,
@@ -191,7 +191,7 @@
                 pltpu.SemaphoreType.DMA((NZ,)),
             ],
         ),
-        compiler_params=pltpu.CompilerParams(vmem_limit_bytes=56 * 2**20),
+        compiler_params=pltpu.CompilerParams(vmem_limit_bytes=26 * 2**20),
         cost_estimate=pl.CostEstimate(
             flops=4 * kinds * key_count * NZ * depth * width,
             bytes_accessed=2 * NZ * depth * (2 * key_count + kinds * width)
@@ -248,7 +248,7 @@
             in_specs=[rows, rows, block_spec(0), block_spec(1)],
             out_specs=[out_spec(n % 2) for n in range(4)],
         ),
-        compiler_params=pltpu.CompilerParams(vmem_limit_bytes=56 * 2**20),
+        compiler_params=pltpu.CompilerParams(vmem_limit_bytes=16 * 2**20),
         cost_estimate=pl.CostEstimate(
             flops=8 * length * depth * steps * width,
             bytes_accessed=2 * (4 * length * depth + 2 * steps * depth * width + 8 * length * width),
@@ -335,10 +335,11 @@
     here = jnp.stack([x, yh * 2 + yl, core, yl, place % NZ]).astype(jnp.int32)
 
     latent_blocks = gather_plane(latents[0])
-    latent_weights = ring_z(to_parity(jnp.stack([w_key, w_value])))
+    shards = to_parity(jnp.stack([w_key, w_value, w_query]))
+    latent_weights = ring_z(shards[:2])
     one_away, two_away = (latent_weights[1], latent_weights[8]), (latent_weights[2], latent_weights[7])
-    query_weights = gather_z(to_parity(after(w_query, *one_away)))
-    out_weights = gather_z(swap_core_parity(after(w_out, *two_away)))
+    query_weights = gather_z(shards[2])
+    out_weights = gather_z(after(swap_core_parity(after(w_out, shards)), *two_away))
 
     normed = layer_norm(text_states[0], norm_gain)
     own_half = pick(normed, core)
@@ -346,10 +347,12 @@
     other_image = over_y(after(token_image, *two_away), 1)
     images = jnp.where(core == yl, token_image, other_image)[0]
 
-    kept, sent = project_queries(here, normed, other_half, query_weights)
-    queries = (kept + swap_cores(sent)).astype(jnp.bfloat16)
     kept, sent = project_latents(here, latent_blocks, latent_weights)
-    keys, values = (kept + swap_cores(sent)).astype(jnp.bfloat16)
+    received = swap_cores(sent)
+    query_kept, query_sent = project_queries(here, normed, other_half, after(query_weights, sent))
+    query_received = swap_cores(query_sent)
+    keys, values = (kept + after(received, query_kept)).astype(jnp.bfloat16)
+    queries = (query_kept + query_received).astype(jnp.bfloat16)
     attended = attend(attention_weights(queries, keys, images), values)
 
     mine = jnp.stack([attended, over_y(attended, 1)])

time: 293 us -> 285 us (0.973)
  local copies, waits for them, and re-layouts: 8.78 us -> 24.9 us
  starting transfers between devices: 61.6 us -> 47.3 us
  Pallas kernels: 39.9 us -> 30.4 us
    unnamed x28 -> x30, local copies, waits for them, and re-layouts: 3.92 us -> 18.9 us
    ppermute x22 -> x21, starting transfers between devices: 61.6 us -> 47.2 us  [permute(): return lax.ppermute(value, AXES, pairs)]
    ppermute x22 -> x21, waiting for transfers between devices: 153 us -> 142 us  [permute(): return lax.ppermute(value, AXES, pairs)]
    all_gather x2, waiting for transfers between devices: 6.38 us -> 15.5 us  [gather_z(): return lax.all_gather(value, 'fsdp', axis=0, axis_index_groups=groups)]
    pallas_call x1, Pallas kernels: 19.1 us -> 15.2 us  [project_latents(): pl.pallas_call(latent_kernel, out_shape=(out, out), grid_spec=pltpu.Prefe...]
    pallas_call x1, Pallas kernels: 6.99 us -> 3.64 us  [partial_sums(): pl.pallas_call(out_kernel, out_shape=[jax.ShapeDtypeStruct((2, length, wi...]
  transfers between devices with their start and end apart: 25 -> 24, of which waited for: 17 -> 16; matrix products, arithmetic and copies ran while one was open for 3% -> 5% of each run, Pallas kernels for 11% -> 9%
where the time goes in v2:
time: 285 us; the launch traced here: 284 us
  waiting for transfers between devices  158 us (55%)
  starting transfers between devices  47.3 us (17%)
  Pallas kernels  30.4 us (11%)
  local copies, waits for them, and re-layouts  24.9 us (9%)
  between operations  14.1 us (5%)
  other arithmetic  6.75 us (2%)
    ppermute x21, waiting for transfers between devices, permute(): return lax.ppermute(value, AXES, pairs)  142 us
    ppermute x21, starting transfers between devices, permute(): return lax.ppermute(value, AXES, pairs)  47.2 us
    unnamed x30, local copies, waits for them, and re-layouts  18.9 us
    all_gather x2, waiting for transfers between devices, gather_z(): return lax.all_gather(value, 'fsdp', axis=0, axis_index_groups=groups)  15.5 us
    pallas_call x1, Pallas kernels, project_latents(): pl.pallas_call(latent_kernel, out_shape=(out, out), grid_spec=pltpu.Prefe...  15.2 us
    pallas_call x1, Pallas kernels, project_queries(): pl.pallas_call(query_kernel, out_shape=(out, out), grid_spec=pltpu.Prefet...  7.07 us
  transfers between devices with their start and end apart: 24, of which 16 were waited for; matrix products, arithmetic and copies ran while one was open for 5% of the time, Pallas kernels for 9%

profile of v2, /device:TPU:8, one launch (start us, length us, event | category | flops | bytes accessed | tf_op | source)
XLA Modules:
  0.0 284.4 jit_solution(11431239878070101778)
XLA Ops:
  8.8 3.7 %collective-permute-start = (bf16[3,512,512]{2,1,0:T(8,128)(2,1)S(1)}, bf16[3,512,512]{2,1,0:T(8,128)(2,1)S(1)}, u32[]{:S(2)}, u32[]{:S(2)}) collective-permute-start(bf16[3,512,512]{2,1,0:T(8,128)(2,1)S(1)} %pad_maximum_fusion), channel_id=1, source_target_pairs={{0,0},{1,17},{2,2},{3,19},{4,4},{5,21},{6,6},{7,23},{8,1},{9,16},{... | collective-permute-start | bytes 4718600 | tf_op jit(solution)/shard_map/ppermute | solution.py:28
  12.6 18.0 %collective-permute-done = bf16[3,512,512]{2,1,0:T(8,128)(2,1)S(1)} collective-permute-done((bf16[3,512,512]{2,1,0:T(8,128)(2,1)S(1)}, bf16[3,512,512]{2,1,0:T(8,128)(2,1)S(1)}, u32[]{:S(2)}, u32[]{:S(2)}) %collective-permute-start) | collective-permute-done | bytes 1572896 | tf_op jit(solution)/shard_map/ppermute | solution.py:28
  34.6 4.0 %collective-permute-start.1 = (bf16[2,512,512]{2,1,0:T(8,128)(2,1)S(1)}, bf16[2,512,512]{2,1,0:T(8,128)(2,1)S(1)}, u32[]{:S(2)}, u32[]{:S(2)}) collective-permute-start(bf16[2,512,512]{2,1,0:T(8,128)(2,1)S(1)} %slice.24.refs_0_), channel_id=1, source_target_pairs={{0,7},{1,0},{2,1},{3,2},{4,3},{5,4},{6,5},{7,6},{8,15},{9,8},{10,9... | collective-permute-start | bytes 3145736 | tf_op jit(solution)/shard_map/ppermute | solution.py:28
  38.6 19.9 %collective-permute-done.4.refs_8_ = bf16[2,512,512]{2,1,0:T(8,128)(2,1)S(1)} collective-permute-done((bf16[2,512,512]{2,1,0:T(8,128)(2,1)S(1)}, bf16[2,512,512]{2,1,0:T(8,128)(2,1)S(1)}, u32[]{:S(2)}, u32[]{:S(2)}) %collective-permute-start.4) | collective-permute-done | bytes 1048608 | tf_op jit(solution)/shard_map/ppermute | solution.py:28
  59.7 3.8 %collective-permute-start.2 = (bf16[2,512,512]{2,1,0:T(8,128)(2,1)S(1)}, bf16[2,512,512]{2,1,0:T(8,128)(2,1)}, u32[]{:S(2)}, u32[]{:S(2)}) collective-permute-start(bf16[2,512,512]{2,1,0:T(8,128)(2,1)S(1)} %collective-permute-done.1.refs_1_), channel_id=1, source_target_pairs={{0,7},{1,0},{2,1},{3,2},{4,3},{5,4},{6,5},{7,6},{8,15},{9,8},{10,9... | collective-permute-start | bytes 3145736 | tf_op jit(solution)/shard_map/ppermute | solution.py:28
  64.4 5.4 %collective-permute-start.15 = (bf16[512,512]{1,0:T(8,128)(2,1)}, bf16[512,512]{1,0:T(8,128)(2,1)}, u32[]{:S(2)}, u32[]{:S(2)}) collective-permute-start(bf16[512,512]{1,0:T(8,128)(2,1)} %param.15), channel_id=1, source_target_pairs={{0,0},{1,16},{2,2},{3,18},{4,4},{5,20},{6,6},{7,22},{8,8},{9,24},{... | collective-permute-start | bytes 1572872 | tf_op jit(solution)/shard_map/ppermute | solution.py:28
  69.8 14.0 %collective-permute-done.5.refs_7_ = bf16[2,512,512]{2,1,0:T(8,128)(2,1)} collective-permute-done((bf16[2,512,512]{2,1,0:T(8,128)(2,1)S(1)}, bf16[2,512,512]{2,1,0:T(8,128)(2,1)}, u32[]{:S(2)}, u32[]{:S(2)}) %collective-permute-start.5) | collective-permute-done | bytes 1048608 | tf_op jit(solution)/shard_map/ppermute | solution.py:28
  88.6 23.1 %collective-permute-done.6.refs_6_ = bf16[2,512,512]{2,1,0:T(8,128)(2,1)S(1)} collective-permute-done((bf16[2,512,512]{2,1,0:T(8,128)(2,1)}, bf16[2,512,512]{2,1,0:T(8,128)(2,1)S(1)}, u32[]{:S(2)}, u32[]{:S(2)}) %collective-permute-start.6) | collective-permute-done | bytes 1048608 | tf_op jit(solution)/shard_map/ppermute | solution.py:28
  114.9 6.3 %collective-permute-done.3.refs_3_ = bf16[2,512,512]{2,1,0:T(8,128)(2,1)S(1)} collective-permute-done((bf16[2,512,512]{2,1,0:T(8,128)(2,1)}, bf16[2,512,512]{2,1,0:T(8,128)(2,1)S(1)}, u32[]{:S(2)}, u32[]{:S(2)}) %collective-permute-start.3) | collective-permute-done | bytes 1048608 | tf_op jit(solution)/shard_map/ppermute | solution.py:28
  122.0 5.8 %collective-permute-start.8 = (bf16[1,512,512]{2,1,0:T(8,128)(2,1)}, bf16[1,512,512]{2,1,0:T(8,128)(2,1)}, u32[]{:S(2)}, u32[]{:S(2)}) collective-permute-start(bf16[1,512,512]{2,1,0:T(8,128)(2,1)} %slice.26), channel_id=1, source_target_pairs={{0,7},{1,0},{2,1},{3,2},{4,3},{5,4},{6,5},{7,6},{8,15},{9,8},{10,9... | collective-permute-start | bytes 1572872 | tf_op jit(solution)/shard_map/ppermute | solution.py:28
  130.2 4.4 %shard_map.92.own_ref = bf16[2,256,4096]{2,1,0:T(8,128)(2,1)S(1)} custom-call(bf16[256,8192]{1,0:T(8,128)(2,1)S(1)} %bitcast.43, f32[1,8192]{1,0:T(1,128)S(1)} %bitcast.44), custom_call_target="tpu_custom_call" | custom-call | flops 16777216 | bytes 8388608 | tf_op jit(solution)/shard_map/pallas_call | solution.py:273
  138.5 4.3 %collective-permute-done.7.refs_4_ = bf16[1,512,512]{2,1,0:T(8,128)(2,1)} collective-permute-done((bf16[1,512,512]{2,1,0:T(8,128)(2,1)}, bf16[1,512,512]{2,1,0:T(8,128)(2,1)}, u32[]{:S(2)}, u32[]{:S(2)}) %collective-permute-start.7) | collective-permute-done | bytes 524320 | tf_op jit(solution)/shard_map/ppermute | solution.py:28
  142.7 5.1 %collective-permute-done.8.refs_5_ = bf16[1,512,512]{2,1,0:T(8,128)(2,1)} collective-permute-done((bf16[1,512,512]{2,1,0:T(8,128)(2,1)}, bf16[1,512,512]{2,1,0:T(8,128)(2,1)}, u32[]{:S(2)}, u32[]{:S(2)}) %collective-permute-start.8) | collective-permute-done | bytes 524320 | tf_op jit(solution)/shard_map/ppermute | solution.py:28
  153.8 15.2 %shard_map.91 = (f32[2,512,512]{2,1,0:T(8,128)S(1)}, f32[2,512,512]{2,1,0:T(8,128)}) custom-call(s32[5]{0:T(128)S(1)} %stack.41.place_ref, bf16[16,512,512]{2,1,0:T(8,128)(2,1)S(1)} %copy-done, bf16[16,512,512]{2,1,0:T(8,128)(2,1)S(1)} %copy-done, bf16[16,512,512]{2,1,0:T(8,128)(2,1)S(1)} %copy-done, bf16[16,512,512]{2,1,0:T(8,128)(2,1)S(1)} %copy-done, ...), custom_call_target="tpu_custom_call" | custom-call | flops 8589934592 | bytes 20971520 | tf_op jit(solution)/shard_map/pallas_call | solution.py:180
  171.1 8.8 %collective-permute-done.11 = s32[1,256]{1,0:T(1,128)S(1)} collective-permute-done((s32[1,256]{1,0:T(1,128)S(1)}, s32[1,256]{1,0:T(1,128)S(1)}, u32[]{:S(2)}, u32[]{:S(2)}) %collective-permute-start.11) | collective-permute-done | bytes 1056 | tf_op jit(solution)/shard_map/ppermute | solution.py:28
  184.6 7.1 %shard_map.93 = (f32[256,512]{1,0:T(8,128)S(1)}, f32[256,512]{1,0:T(8,128)S(1)}) custom-call(s32[5]{0:T(128)S(1)} %stack.41.place_ref, bf16[2,256,4096]{2,1,0:T(8,128)(2,1)S(1)} %copy-done.2, bf16[256,4096]{1,0:T(8,128)(2,1)} %collective-permute-done.10.other_ref, bf16[8,512,512]{2,1,0:T(8,128)(2,1)S(1)} %copy-done.5), custom_call_target="tpu_custom_call" | custom-call | flops 2147483648 | bytes 9437184 | tf_op jit(solution)/shard_map/pallas_call | solution.py:145
  199.3 8.1 %collective-permute-done.13 = bf16[256,512]{1,0:T(8,128)(2,1)S(1)} collective-permute-done((bf16[256,512]{1,0:T(8,128)(2,1)S(1)}, bf16[256,512]{1,0:T(8,128)(2,1)S(1)}, u32[]{:S(2)}, u32[]{:S(2)}) %collective-permute-start.13) | collective-permute-done | bytes 262176 | tf_op jit(solution)/shard_map/ppermute | solution.py:28
  207.5 15.5 %all-gather.9.cloned.1.call-done = bf16[4096,512]{1,0:T(8,128)(2,1)} async-done(((bf16[512,512]{1,0:T(8,128)(2,1)}), bf16[4096,512]{1,0:T(8,128)(2,1)}) %all-gather.9.cloned.1.call-update) | async-done | bytes 4194320 | tf_op jit(solution)/shard_map/all_gather | solution.py:73
  225.2 3.6 %shard_map.94 = (bf16[2,256,512]{2,1,0:T(8,128)(2,1)S(1)}, bf16[2,256,512]{2,1,0:T(8,128)(2,1)S(1)}, bf16[2,256,512]{2,1,0:T(8,128)(2,1)S(1)}, bf16[2,256,512]{2,1,0:T(8,128)(2,1)S(1)}) custom-call(s32[5]{0:T(128)S(1)} %stack.41.place_ref, bf16[2,256,512]{2,1,0:T(8,128)(2,1)S(1)} %pad_maximum_fusion.1.mine_ref, ...), custom_call_target="tpu_custom_call" | custom-call | flops 2147483648 | bytes 7340032 | tf_op jit(solution)/shard_map/pallas_call | solution.py:242
  233.6 10.1 %collective-permute-done.16 = bf16[2,256,512]{2,1,0:T(8,128)(2,1)S(1)} collective-permute-done((bf16[2,256,512]{2,1,0:T(8,128)(2,1)S(1)}, bf16[2,256,512]{2,1,0:T(8,128)(2,1)S(1)}, u32[]{:S(2)}, u32[]{:S(2)}) %collective-permute-start.16) | collective-permute-done | bytes 524320 | tf_op jit(solution)/shard_map/ppermute | solution.py:28
  243.7 12.3 %collective-permute-done.17 = bf16[2,256,512]{2,1,0:T(8,128)(2,1)S(1)} collective-permute-done((bf16[2,256,512]{2,1,0:T(8,128)(2,1)S(1)}, bf16[2,256,512]{2,1,0:T(8,128)(2,1)S(1)}, u32[]{:S(2)}, u32[]{:S(2)}) %collective-permute-start.17) | collective-permute-done | bytes 524320 | tf_op jit(solution)/shard_map/ppermute | solution.py:28
  260.9 5.2 %collective-permute-start.20 = (bf16[256,512]{1,0:T(8,128)(2,1)S(1)}, bf16[256,512]{1,0:T(8,128)(2,1)S(1)}, u32[]{:S(2)}, u32[]{:S(2)}) collective-permute-start(bf16[256,512]{1,0:T(8,128)(2,1)S(1)} %get-tuple-element.36), channel_id=1, source_target_pairs={{0,32},{1,33},{2,34},{3,35},{4,36},{5,37},{6,38},{7,39},{8,160},{9... | collective-permute-start | bytes 786440 | tf_op jit(solution)/shard_map/ppermute | solution.py:28
  266.7 5.8 %collective-permute-done.19 = bf16[256,512]{1,0:T(8,128)(2,1)S(1)} collective-permute-done((bf16[256,512]{1,0:T(8,128)(2,1)S(1)}, bf16[256,512]{1,0:T(8,128)(2,1)S(1)}, u32[]{:S(2)}, u32[]{:S(2)}) %collective-permute-start.19) | collective-permute-done | bytes 262176 | tf_op jit(solution)/shard_map/ppermute | solution.py:28
  272.5 3.6 %collective-permute-done.20 = bf16[256,512]{1,0:T(8,128)(2,1)S(1)} collective-permute-done((bf16[256,512]{1,0:T(8,128)(2,1)S(1)}, bf16[256,512]{1,0:T(8,128)(2,1)S(1)}, u32[]{:S(2)}, u32[]{:S(2)}) %collective-permute-start.20) | collective-permute-done | bytes 262176 | tf_op jit(solution)/shard_map/ppermute | solution.py:28
  (87 shorter events, 57.4 us)
Async XLA Ops:
  6.5 141.3 %all-gather.5.cloned.1.call-start = ((), (), s32[]{:S(2)}) async-start(), calls=%async_computation | async-start | bytes 8912896 | tf_op jit(solution)/shard_map/all_gather | solution.py:86
  7.3 173.0 %all-gather.7.cloned.1.call-start = ((), (), s32[]{:S(2)}) async-start(), calls=%async_computation.1 | async-start | bytes 4718592 | tf_op jit(solution)/shard_map/all_gather | solution.py:73
  8.8 21.7 %collective-permute-start = (bf16[3,512,512]{2,1,0:T(8,128)(2,1)S(1)}, bf16[3,512,512]{2,1,0:T(8,128)(2,1)S(1)}, u32[]{:S(2)}, u32[]{:S(2)}) collective-permute-start(bf16[3,512,512]{2,1,0:T(8,128)(2,1)S(1)} %pad_maximum_fusion), channel_id=1, source_target_pairs={{0,0},{1,17},{2,2},{3,19},{4,4},{5,21},{6,6},{7,23},{8,1},{9,16},{... | collective-permute-start | bytes 4718600 | tf_op jit(solution)/shard_map/ppermute | solution.py:28
  31.4 191.6 %all-gather.9.cloned.1.call-start = ((), (), s32[]{:S(2)}) async-start(), calls=%async_computation.2 | async-start | bytes 4718592 | tf_op jit(solution)/shard_map/all_gather | solution.py:73
  31.5 27.0 %collective-permute-start.4 = (bf16[2,512,512]{2,1,0:T(8,128)(2,1)S(1)}, bf16[2,512,512]{2,1,0:T(8,128)(2,1)S(1)}, u32[]{:S(2)}, u32[]{:S(2)}) collective-permute-start(bf16[2,512,512]{2,1,0:T(8,128)(2,1)S(1)} %slice.24.refs_0_), channel_id=1, source_target_pairs={{0,1},{1,2},{2,3},{3,4},{4,5},{5,6},{6,7},{7,0},{8,9},{9,10},{10,1... | collective-permute-start | bytes 3145736 | tf_op jit(solution)/shard_map/ppermute | solution.py:28
  34.6 25.1 %collective-permute-start.1 = (bf16[2,512,512]{2,1,0:T(8,128)(2,1)S(1)}, bf16[2,512,512]{2,1,0:T(8,128)(2,1)S(1)}, u32[]{:S(2)}, u32[]{:S(2)}) collective-permute-start(bf16[2,512,512]{2,1,0:T(8,128)(2,1)S(1)} %slice.24.refs_0_), channel_id=1, source_target_pairs={{0,7},{1,0},{2,1},{3,2},{4,3},{5,4},{6,5},{7,6},{8,15},{9,8},{10,9... | collective-permute-start | bytes 3145736 | tf_op jit(solution)/shard_map/ppermute | solution.py:28
  58.5 25.3 %collective-permute-start.5 = (bf16[2,512,512]{2,1,0:T(8,128)(2,1)S(1)}, bf16[2,512,512]{2,1,0:T(8,128)(2,1)}, u32[]{:S(2)}, u32[]{:S(2)}) collective-permute-start(bf16[2,512,512]{2,1,0:T(8,128)(2,1)S(1)} %collective-permute-done.4.refs_8_), channel_id=1, source_target_pairs={{0,1},{1,2},{2,3},{3,4},{4,5},{5,6},{6,7},{7,0},{8,9},{9,10},{10,1... | collective-permute-start | bytes 3145736 | tf_op jit(solution)/shard_map/ppermute | solution.py:28
  59.7 25.5 %collective-permute-start.2 = (bf16[2,512,512]{2,1,0:T(8,128)(2,1)S(1)}, bf16[2,512,512]{2,1,0:T(8,128)(2,1)}, u32[]{:S(2)}, u32[]{:S(2)}) collective-permute-start(bf16[2,512,512]{2,1,0:T(8,128)(2,1)S(1)} %collective-permute-done.1.refs_1_), channel_id=1, source_target_pairs={{0,7},{1,0},{2,1},{3,2},{4,3},{5,4},{6,5},{7,6},{8,15},{9,8},{10,9... | collective-permute-start | bytes 3145736 | tf_op jit(solution)/shard_map/ppermute | solution.py:28
  64.4 24.2 %collective-permute-start.15 = (bf16[512,512]{1,0:T(8,128)(2,1)}, bf16[512,512]{1,0:T(8,128)(2,1)}, u32[]{:S(2)}, u32[]{:S(2)}) collective-permute-start(bf16[512,512]{1,0:T(8,128)(2,1)} %param.15), channel_id=1, source_target_pairs={{0,0},{1,16},{2,2},{3,18},{4,4},{5,20},{6,6},{7,22},{8,8},{9,24},{... | collective-permute-start | bytes 1572872 | tf_op jit(solution)/shard_map/ppermute | solution.py:28
  83.8 27.9 %collective-permute-start.6 = (bf16[2,512,512]{2,1,0:T(8,128)(2,1)}, bf16[2,512,512]{2,1,0:T(8,128)(2,1)S(1)}, u32[]{:S(2)}, u32[]{:S(2)}) collective-permute-start(bf16[2,512,512]{2,1,0:T(8,128)(2,1)} %collective-permute-done.5.refs_7_), channel_id=1, source_target_pairs={{0,1},{1,2},{2,3},{3,4},{4,5},{5,6},{6,7},{7,0},{8,9},{9,10},{10,1... | collective-permute-start | bytes 3145736 | tf_op jit(solution)/shard_map/ppermute | solution.py:28
  85.2 36.0 %collective-permute-start.3 = (bf16[2,512,512]{2,1,0:T(8,128)(2,1)}, bf16[2,512,512]{2,1,0:T(8,128)(2,1)S(1)}, u32[]{:S(2)}, u32[]{:S(2)}) collective-permute-start(bf16[2,512,512]{2,1,0:T(8,128)(2,1)} %collective-permute-done.2.refs_2_), channel_id=1, source_target_pairs={{0,7},{1,0},{2,1},{3,2},{4,3},{5,4},{6,5},{7,6},{8,15},{9,8},{10,9... | collective-permute-start | bytes 3145736 | tf_op jit(solution)/shard_map/ppermute | solution.py:28
  112.5 30.2 %collective-permute-start.7 = (bf16[1,512,512]{2,1,0:T(8,128)(2,1)}, bf16[1,512,512]{2,1,0:T(8,128)(2,1)}, u32[]{:S(2)}, u32[]{:S(2)}) collective-permute-start(bf16[1,512,512]{2,1,0:T(8,128)(2,1)} %slice.25), channel_id=1, source_target_pairs={{0,1},{1,2},{2,3},{3,4},{4,5},{5,6},{6,7},{7,0},{8,9},{9,10},{10,1... | collective-permute-start | bytes 1572872 | tf_op jit(solution)/shard_map/ppermute | solution.py:28
  122.0 25.8 %collective-permute-start.8 = (bf16[1,512,512]{2,1,0:T(8,128)(2,1)}, bf16[1,512,512]{2,1,0:T(8,128)(2,1)}, u32[]{:S(2)}, u32[]{:S(2)}) collective-permute-start(bf16[1,512,512]{2,1,0:T(8,128)(2,1)} %slice.26), channel_id=1, source_target_pairs={{0,7},{1,0},{2,1},{3,2},{4,3},{5,4},{6,5},{7,6},{8,15},{9,8},{10,9... | collective-permute-start | bytes 1572872 | tf_op jit(solution)/shard_map/ppermute | solution.py:28
  137.4 42.9 %collective-permute-start.10 = (bf16[256,4096]{1,0:T(8,128)(2,1)}, bf16[256,4096]{1,0:T(8,128)(2,1)}, u32[]{:S(2)}, u32[]{:S(2)}) collective-permute-start(bf16[256,4096]{1,0:T(8,128)(2,1)} %dynamic-slice_bitcast_fusion), channel_id=1, source_target_pairs={{0,8},{1,9},{2,10},{3,11},{4,12},{5,13},{6,14},{7,15},{8,0},{9,1},... | collective-permute-start | bytes 6291464 | tf_op jit(solution)/shard_map/ppermute | solution.py:28
  170.3 21.5 %collective-permute-start.9 = (f32[2,512,512]{2,1,0:T(8,128)}, f32[2,512,512]{2,1,0:T(8,128)}, u32[]{:S(2)}, u32[]{:S(2)}) collective-permute-start(f32[2,512,512]{2,1,0:T(8,128)} %get-tuple-element.20), channel_id=1, source_target_pairs={{0,16},{1,17},{2,18},{3,19},{4,20},{5,21},{6,22},{7,23},{8,24},{9,... | collective-permute-start | bytes 6291464 | tf_op jit(solution)/shard_map/ppermute | solution.py:28
  170.3 9.5 %collective-permute-start.11 = (s32[1,256]{1,0:T(1,128)S(1)}, s32[1,256]{1,0:T(1,128)S(1)}, u32[]{:S(2)}, u32[]{:S(2)}) collective-permute-start(s32[1,256]{1,0:T(1,128)S(1)} %copy-done.14), channel_id=1, source_target_pairs={{0,8},{1,9},{2,10},{3,11},{4,12},{5,13},{6,14},{7,15},{8,0},{9,1},... | collective-permute-start | bytes 3080 | tf_op jit(solution)/shard_map/ppermute | solution.py:28
  191.7 3.3 %collective-permute-start.12 = (f32[256,512]{1,0:T(8,128)S(1)}, f32[256,512]{1,0:T(8,128)}, u32[]{:S(2)}, u32[]{:S(2)}) collective-permute-start(f32[256,512]{1,0:T(8,128)S(1)} %get-tuple-element.26), channel_id=1, source_target_pairs={{0,16},{1,17},{2,18},{3,19},{4,20},{5,21},{6,22},{7,23},{8,24},{9,... | collective-permute-start | bytes 1572872 | tf_op jit(solution)/shard_map/ppermute | solution.py:28
  198.6 8.8 %collective-permute-start.13 = (bf16[256,512]{1,0:T(8,128)(2,1)S(1)}, bf16[256,512]{1,0:T(8,128)(2,1)S(1)}, u32[]{:S(2)}, u32[]{:S(2)}) collective-permute-start(bf16[256,512]{1,0:T(8,128)(2,1)S(1)} %copy.27), channel_id=1, source_target_pairs={{0,8},{1,9},{2,10},{3,11},{4,12},{5,13},{6,14},{7,15},{8,0},{9,1},... | collective-permute-start | bytes 786440 | tf_op jit(solution)/shard_map/ppermute | solution.py:28
  207.4 15.6 %collective-permute-start.14 = (bf16[2,256,512]{2,1,0:T(8,128)(2,1)S(1)}, bf16[2,256,512]{2,1,0:T(8,128)(2,1)S(1)}, u32[]{:S(2)}, u32[]{:S(2)}) collective-permute-start(bf16[2,256,512]{2,1,0:T(8,128)(2,1)S(1)} %pad_maximum_fusion.1.mine_ref), channel_id=1, source_target_pairs={{0,16},{1,17},{2,18},{3,19},{4,20},{5,21},{6,22},{7,23},{8,24},{9,... | collective-permute-start | bytes 1572872 | tf_op jit(solution)/shard_map/ppermute | solution.py:28
  228.8 14.9 %collective-permute-start.16 = (bf16[2,256,512]{2,1,0:T(8,128)(2,1)S(1)}, bf16[2,256,512]{2,1,0:T(8,128)(2,1)S(1)}, u32[]{:S(2)}, u32[]{:S(2)}) collective-permute-start(bf16[2,256,512]{2,1,0:T(8,128)(2,1)S(1)} %get-tuple-element.30), channel_id=1, source_target_pairs={{0,64},{1,65},{2,66},{3,67},{4,68},{5,69},{6,70},{7,71},{8,72},{9,... | collective-permute-start | bytes 1572872 | tf_op jit(solution)/shard_map/ppermute | solution.py:28
  230.4 25.7 %collective-permute-start.17 = (bf16[2,256,512]{2,1,0:T(8,128)(2,1)S(1)}, bf16[2,256,512]{2,1,0:T(8,128)(2,1)S(1)}, u32[]{:S(2)}, u32[]{:S(2)}) collective-permute-start(bf16[2,256,512]{2,1,0:T(8,128)(2,1)S(1)} %get-tuple-element.31), channel_id=1, source_target_pairs={{0,128},{1,129},{2,130},{3,131},{4,132},{5,133},{6,134},{7,135},{8... | collective-permute-start | bytes 1572872 | tf_op jit(solution)/shard_map/ppermute | solution.py:28
  233.1 25.5 %collective-permute-start.18 = (bf16[2,256,512]{2,1,0:T(8,128)(2,1)S(1)}, bf16[2,256,512]{2,1,0:T(8,128)(2,1)S(1)}, u32[]{:S(2)}, u32[]{:S(2)}) collective-permute-start(bf16[2,256,512]{2,1,0:T(8,128)(2,1)S(1)} %get-tuple-element.32), channel_id=1, source_target_pairs={{0,192},{1,193},{2,194},{3,195},{4,196},{5,197},{6,198},{7,199},{8... | collective-permute-start | bytes 1572872 | tf_op jit(solution)/shard_map/ppermute | solution.py:28
  258.9 13.6 %collective-permute-start.19 = (bf16[256,512]{1,0:T(8,128)(2,1)S(1)}, bf16[256,512]{1,0:T(8,128)(2,1)S(1)}, u32[]{:S(2)}, u32[]{:S(2)}) collective-permute-start(bf16[256,512]{1,0:T(8,128)(2,1)S(1)} %get-tuple-element.35), channel_id=1, source_target_pairs={{0,0},{1,1},{2,2},{3,3},{4,4},{5,5},{6,6},{7,7},{8,128},{9,129},{1... | collective-permute-start | bytes 786440 | tf_op jit(solution)/shard_map/ppermute | solution.py:28
  260.9 15.2 %collective-permute-start.20 = (bf16[256,512]{1,0:T(8,128)(2,1)S(1)}, bf16[256,512]{1,0:T(8,128)(2,1)S(1)}, u32[]{:S(2)}, u32[]{:S(2)}) collective-permute-start(bf16[256,512]{1,0:T(8,128)(2,1)S(1)} %get-tuple-element.36), channel_id=1, source_target_pairs={{0,32},{1,33},{2,34},{3,35},{4,36},{5,37},{6,38},{7,39},{8,160},{9... | collective-permute-start | bytes 786440 | tf_op jit(solution)/shard_map/ppermute | solution.py:28
  (15 other events, 162.8 us)
Sparse Core Ops, SparseCore 0:
  9.8 83.0 all-gather.4
  94.7 69.6 all-gather.6
  166.2 56.7 all-gather.8

commit v3 on v2

--- a/solution.py
+++ b/solution.py
@@ -203,6 +203,7 @@
 
 def out_kernel(place_ref, mine_ref, theirs_ref, near_ref, far_ref, *parts):
     core, x_high = place_ref[2], place_ref[0] // 2
+    cut = near_ref.shape[1] // 2
 
     def product(ref):
         return (
@@ -217,8 +218,10 @@
 
         @pl.when(pl.program_id(0) // 2 == n)
         def _():
-            parts[n][...] = near
-            parts[2 + n][...] = far
+            for half in range(2):
+                columns = slice(half * cut, (half + 1) * cut)
+                parts[4 * half + n][...] = near[:, columns]
+                parts[4 * half + 2 + n][...] = far[:, columns]
 
 
 def partial_sums(place, mine, theirs, blocks):
@@ -237,16 +240,16 @@
         def index(s, p):
             return (jnp.where(s // 2 == n, s % 2, jnp.where(s // 2 < n, 0, 1)), 0, 0)
 
-        return pl.BlockSpec((None, length, width), index)
+        return pl.BlockSpec((None, length, width // 2), index)
 
     return pl.pallas_call(
         out_kernel,
-        out_shape=[jax.ShapeDtypeStruct((2, length, width), jnp.bfloat16)] * 4,
+        out_shape=[jax.ShapeDtypeStruct((2, length, width // 2), jnp.bfloat16)] * 8,
         grid_spec=pltpu.PrefetchScalarGridSpec(
             num_scalar_prefetch=1,
             grid=(steps,),
             in_specs=[rows, rows, block_spec(0), block_spec(1)],
-            out_specs=[out_spec(n % 2) for n in range(4)],
+            out_specs=[out_spec(n % 2) for n in range(8)],
         ),
         compiler_params=pltpu.CompilerParams(vmem_limit_bytes=16 * 2**20),
         cost_estimate=pl.CostEstimate(
@@ -357,8 +360,11 @@
 
     mine = jnp.stack([attended, over_y(attended, 1)])
     parts = partial_sums(here, mine, swap_cores(mine), out_weights)
-    near = total(parts[0], [over_x(parts[r], r) for r in (1, 2, 3)]).astype(jnp.bfloat16)
-    projected = total(to_final(near[0], 0), [to_final(near[1], 1)])
+    halves = []
+    for own, *others in (parts[:4], parts[4:]):
+        near = total(own, [over_x(others[r - 1], r) for r in (1, 2, 3)]).astype(jnp.bfloat16)
+        halves.append(total(to_final(near[0], 0), [to_final(near[1], 1)]))
+    projected = jnp.concatenate(halves, axis=1)
     own_text = lax.dynamic_slice_in_dim(text_states[0], section * width, width, 1)
     mixed = own_text.astype(jnp.float32) + jnp.tanh(xattn_gate[0]) * projected
     return mixed.astype(jnp.bfloat16)[None]

time: 285 us -> 283 us (level)
  waiting for transfers between devices: 158 us -> 141 us
  starting transfers between devices: 47.3 us -> 60.8 us
    ppermute x21 -> x26, waiting for transfers between devices: 142 us -> 125 us  [permute(): return lax.ppermute(value, AXES, pairs)]
    ppermute x21 -> x26, starting transfers between devices: 47.2 us -> 60.8 us  [permute(): return lax.ppermute(value, AXES, pairs)]
  transfers between devices with their start and end apart: 24 -> 29, of which waited for: 16 -> 16; matrix products, arithmetic and copies ran while one was open for 5% -> 5% of each run, Pallas kernels for 9% -> 10%
where the time goes in v3:
time: 283 us; the launch traced here: 281 us
  waiting for transfers between devices  141 us (50%)
  starting transfers between devices  60.8 us (21%)
  Pallas kernels  30.3 us (11%)
  local copies, waits for them, and re-layouts  24.9 us (9%)
  between operations  14.1 us (5%)
  other arithmetic  6.78 us (2%)
    ppermute x26, waiting for transfers between devices, permute(): return lax.ppermute(value, AXES, pairs)  125 us
    ppermute x26, starting transfers between devices, permute(): return lax.ppermute(value, AXES, pairs)  60.8 us
    unnamed x30, local copies, waits for them, and re-layouts  18.9 us
    all_gather x2, waiting for transfers between devices, gather_z(): return lax.all_gather(value, 'fsdp', axis=0, axis_index_groups=groups)  15.5 us
    pallas_call x1, Pallas kernels, project_latents(): pl.pallas_call(latent_kernel, out_shape=(out, out), grid_spec=pltpu.Prefe...  15.2 us
    pallas_call x1, Pallas kernels, project_queries(): pl.pallas_call(query_kernel, out_shape=(out, out), grid_spec=pltpu.Prefet...  7.07 us
  transfers between devices with their start and end apart: 29, of which 16 were waited for; matrix products, arithmetic and copies ran while one was open for 5% of the time, Pallas kernels for 10%

profile of v3, /device:TPU:8, one launch (start us, length us, event | category | flops | bytes accessed | tf_op | source)
XLA Modules:
  0.0 280.9 jit_solution(10411970386835808381)
XLA Ops:
  8.8 3.7 %collective-permute-start = (bf16[3,512,512]{2,1,0:T(8,128)(2,1)S(1)}, bf16[3,512,512]{2,1,0:T(8,128)(2,1)S(1)}, u32[]{:S(2)}, u32[]{:S(2)}) collective-permute-start(bf16[3,512,512]{2,1,0:T(8,128)(2,1)S(1)} %pad_maximum_fusion), channel_id=1, source_target_pairs={{0,0},{1,17},{2,2},{3,19},{4,4},{5,21},{6,6},{7,23},{8,1},{9,16},{... | collective-permute-start | bytes 4718600 | tf_op jit(solution)/shard_map/ppermute | solution.py:28
  12.6 18.0 %collective-permute-done = bf16[3,512,512]{2,1,0:T(8,128)(2,1)S(1)} collective-permute-done((bf16[3,512,512]{2,1,0:T(8,128)(2,1)S(1)}, bf16[3,512,512]{2,1,0:T(8,128)(2,1)S(1)}, u32[]{:S(2)}, u32[]{:S(2)}) %collective-permute-start) | collective-permute-done | bytes 1572896 | tf_op jit(solution)/shard_map/ppermute | solution.py:28
  34.6 4.0 %collective-permute-start.1 = (bf16[2,512,512]{2,1,0:T(8,128)(2,1)S(1)}, bf16[2,512,512]{2,1,0:T(8,128)(2,1)S(1)}, u32[]{:S(2)}, u32[]{:S(2)}) collective-permute-start(bf16[2,512,512]{2,1,0:T(8,128)(2,1)S(1)} %slice.32.refs_0_), channel_id=1, source_target_pairs={{0,7},{1,0},{2,1},{3,2},{4,3},{5,4},{6,5},{7,6},{8,15},{9,8},{10,9... | collective-permute-start | bytes 3145736 | tf_op jit(solution)/shard_map/ppermute | solution.py:28
  38.6 19.9 %collective-permute-done.4.refs_8_ = bf16[2,512,512]{2,1,0:T(8,128)(2,1)S(1)} collective-permute-done((bf16[2,512,512]{2,1,0:T(8,128)(2,1)S(1)}, bf16[2,512,512]{2,1,0:T(8,128)(2,1)S(1)}, u32[]{:S(2)}, u32[]{:S(2)}) %collective-permute-start.4) | collective-permute-done | bytes 1048608 | tf_op jit(solution)/shard_map/ppermute | solution.py:28
  59.7 3.8 %collective-permute-start.2 = (bf16[2,512,512]{2,1,0:T(8,128)(2,1)S(1)}, bf16[2,512,512]{2,1,0:T(8,128)(2,1)}, u32[]{:S(2)}, u32[]{:S(2)}) collective-permute-start(bf16[2,512,512]{2,1,0:T(8,128)(2,1)S(1)} %collective-permute-done.1.refs_1_), channel_id=1, source_target_pairs={{0,7},{1,0},{2,1},{3,2},{4,3},{5,4},{6,5},{7,6},{8,15},{9,8},{10,9... | collective-permute-start | bytes 3145736 | tf_op jit(solution)/shard_map/ppermute | solution.py:28
  64.5 5.4 %collective-permute-start.15 = (bf16[512,512]{1,0:T(8,128)(2,1)}, bf16[512,512]{1,0:T(8,128)(2,1)}, u32[]{:S(2)}, u32[]{:S(2)}) collective-permute-start(bf16[512,512]{1,0:T(8,128)(2,1)} %param.15), channel_id=1, source_target_pairs={{0,0},{1,16},{2,2},{3,18},{4,4},{5,20},{6,6},{7,22},{8,8},{9,24},{... | collective-permute-start | bytes 1572872 | tf_op jit(solution)/shard_map/ppermute | solution.py:28
  69.9 13.9 %collective-permute-done.5.refs_7_ = bf16[2,512,512]{2,1,0:T(8,128)(2,1)} collective-permute-done((bf16[2,512,512]{2,1,0:T(8,128)(2,1)S(1)}, bf16[2,512,512]{2,1,0:T(8,128)(2,1)}, u32[]{:S(2)}, u32[]{:S(2)}) %collective-permute-start.5) | collective-permute-done | bytes 1048608 | tf_op jit(solution)/shard_map/ppermute | solution.py:28
  88.6 23.1 %collective-permute-done.6.refs_6_ = bf16[2,512,512]{2,1,0:T(8,128)(2,1)S(1)} collective-permute-done((bf16[2,512,512]{2,1,0:T(8,128)(2,1)}, bf16[2,512,512]{2,1,0:T(8,128)(2,1)S(1)}, u32[]{:S(2)}, u32[]{:S(2)}) %collective-permute-start.6) | collective-permute-done | bytes 1048608 | tf_op jit(solution)/shard_map/ppermute | solution.py:28
  114.9 6.3 %collective-permute-done.3.refs_3_ = bf16[2,512,512]{2,1,0:T(8,128)(2,1)S(1)} collective-permute-done((bf16[2,512,512]{2,1,0:T(8,128)(2,1)}, bf16[2,512,512]{2,1,0:T(8,128)(2,1)S(1)}, u32[]{:S(2)}, u32[]{:S(2)}) %collective-permute-start.3) | collective-permute-done | bytes 1048608 | tf_op jit(solution)/shard_map/ppermute | solution.py:28
  122.1 5.8 %collective-permute-start.8 = (bf16[1,512,512]{2,1,0:T(8,128)(2,1)}, bf16[1,512,512]{2,1,0:T(8,128)(2,1)}, u32[]{:S(2)}, u32[]{:S(2)}) collective-permute-start(bf16[1,512,512]{2,1,0:T(8,128)(2,1)} %slice.34), channel_id=1, source_target_pairs={{0,7},{1,0},{2,1},{3,2},{4,3},{5,4},{6,5},{7,6},{8,15},{9,8},{10,9... | collective-permute-start | bytes 1572872 | tf_op jit(solution)/shard_map/ppermute | solution.py:28
  130.2 4.4 %shard_map.92.own_ref = bf16[2,256,4096]{2,1,0:T(8,128)(2,1)S(1)} custom-call(bf16[256,8192]{1,0:T(8,128)(2,1)S(1)} %bitcast.46, f32[1,8192]{1,0:T(1,128)S(1)} %bitcast.47), custom_call_target="tpu_custom_call" | custom-call | flops 16777216 | bytes 8388608 | tf_op jit(solution)/shard_map/pallas_call | solution.py:276
  138.4 4.3 %collective-permute-done.7.refs_4_ = bf16[1,512,512]{2,1,0:T(8,128)(2,1)} collective-permute-done((bf16[1,512,512]{2,1,0:T(8,128)(2,1)}, bf16[1,512,512]{2,1,0:T(8,128)(2,1)}, u32[]{:S(2)}, u32[]{:S(2)}) %collective-permute-start.7) | collective-permute-done | bytes 524320 | tf_op jit(solution)/shard_map/ppermute | solution.py:28
  142.7 5.1 %collective-permute-done.8.refs_5_ = bf16[1,512,512]{2,1,0:T(8,128)(2,1)} collective-permute-done((bf16[1,512,512]{2,1,0:T(8,128)(2,1)}, bf16[1,512,512]{2,1,0:T(8,128)(2,1)}, u32[]{:S(2)}, u32[]{:S(2)}) %collective-permute-start.8) | collective-permute-done | bytes 524320 | tf_op jit(solution)/shard_map/ppermute | solution.py:28
  153.8 15.2 %shard_map.91 = (f32[2,512,512]{2,1,0:T(8,128)S(1)}, f32[2,512,512]{2,1,0:T(8,128)}) custom-call(s32[5]{0:T(128)S(1)} %stack.41.place_ref, bf16[16,512,512]{2,1,0:T(8,128)(2,1)S(1)} %copy-done, bf16[16,512,512]{2,1,0:T(8,128)(2,1)S(1)} %copy-done, bf16[16,512,512]{2,1,0:T(8,128)(2,1)S(1)} %copy-done, bf16[16,512,512]{2,1,0:T(8,128)(2,1)S(1)} %copy-done, ...), custom_call_target="tpu_custom_call" | custom-call | flops 8589934592 | bytes 20971520 | tf_op jit(solution)/shard_map/pallas_call | solution.py:180
  171.1 8.7 %collective-permute-done.11 = s32[1,256]{1,0:T(1,128)S(1)} collective-permute-done((s32[1,256]{1,0:T(1,128)S(1)}, s32[1,256]{1,0:T(1,128)S(1)}, u32[]{:S(2)}, u32[]{:S(2)}) %collective-permute-start.11) | collective-permute-done | bytes 1056 | tf_op jit(solution)/shard_map/ppermute | solution.py:28
  184.6 7.1 %shard_map.93 = (f32[256,512]{1,0:T(8,128)S(1)}, f32[256,512]{1,0:T(8,128)S(1)}) custom-call(s32[5]{0:T(128)S(1)} %stack.41.place_ref, bf16[2,256,4096]{2,1,0:T(8,128)(2,1)S(1)} %copy-done.2, bf16[256,4096]{1,0:T(8,128)(2,1)} %collective-permute-done.10.other_ref, bf16[8,512,512]{2,1,0:T(8,128)(2,1)S(1)} %copy-done.5), custom_call_target="tpu_custom_call" | custom-call | flops 2147483648 | bytes 9437184 | tf_op jit(solution)/shard_map/pallas_call | solution.py:145
  199.3 8.1 %collective-permute-done.13 = bf16[256,512]{1,0:T(8,128)(2,1)S(1)} collective-permute-done((bf16[256,512]{1,0:T(8,128)(2,1)S(1)}, bf16[256,512]{1,0:T(8,128)(2,1)S(1)}, u32[]{:S(2)}, u32[]{:S(2)}) %collective-permute-start.13) | collective-permute-done | bytes 262176 | tf_op jit(solution)/shard_map/ppermute | solution.py:28
  207.5 15.5 %all-gather.9.cloned.1.call-done = bf16[4096,512]{1,0:T(8,128)(2,1)} async-done(((bf16[512,512]{1,0:T(8,128)(2,1)}), bf16[4096,512]{1,0:T(8,128)(2,1)}) %all-gather.9.cloned.1.call-update) | async-done | bytes 4194320 | tf_op jit(solution)/shard_map/all_gather | solution.py:73
  225.2 3.6 %shard_map.94 = (bf16[2,256,256]{2,1,0:T(8,128)(2,1)S(1)}, bf16[2,256,256]{2,1,0:T(8,128)(2,1)S(1)}, bf16[2,256,256]{2,1,0:T(8,128)(2,1)S(1)}, bf16[2,256,256]{2...) custom-call(s32[5]{0:T(128)S(1)} %stack.41.place_ref, ...), custom_call_target="tpu_custom_call" | custom-call | flops 2147483648 | bytes 7340032 | tf_op jit(solution)/shard_map/pallas_call | solution.py:245
  234.7 3.9 %collective-permute-start.22 = (bf16[2,256,256]{2,1,0:T(8,128)(2,1)S(1)}, bf16[2,256,256]{2,1,0:T(8,128)(2,1)S(1)}, u32[]{:S(2)}, u32[]{:S(2)}) collective-permute-start(bf16[2,256,256]{2,1,0:T(8,128)(2,1)S(1)} %get-tuple-element.39), channel_id=1, source_target_pairs={{0,128},{1,129},{2,130},{3,131},{4,132},{5,133},{6,134},{7,135},{8... | collective-permute-start | bytes 786440 | tf_op jit(solution)/shard_map/ppermute | solution.py:28
  240.8 5.1 %collective-permute-done.17 = bf16[2,256,256]{2,1,0:T(8,128)(2,1)S(1)} collective-permute-done((bf16[2,256,256]{2,1,0:T(8,128)(2,1)S(1)}, bf16[2,256,256]{2,1,0:T(8,128)(2,1)S(1)}, u32[]{:S(2)}, u32[]{:S(2)}) %collective-permute-start.17) | collective-permute-done | bytes 262176 | tf_op jit(solution)/shard_map/ppermute | solution.py:28
  251.2 5.2 %collective-permute-start.20 = (bf16[256,256]{1,0:T(8,128)(2,1)S(1)}, bf16[256,256]{1,0:T(8,128)(2,1)S(1)}, u32[]{:S(2)}, u32[]{:S(2)}) collective-permute-start(bf16[256,256]{1,0:T(8,128)(2,1)S(1)} %get-tuple-element.44), channel_id=1, source_target_pairs={{0,32},{1,33},{2,34},{3,35},{4,36},{5,37},{6,38},{7,39},{8,160},{9... | collective-permute-start | bytes 393224 | tf_op jit(solution)/shard_map/ppermute | solution.py:28
  256.4 4.6 %collective-permute-done.23 = bf16[2,256,256]{2,1,0:T(8,128)(2,1)S(1)} collective-permute-done((bf16[2,256,256]{2,1,0:T(8,128)(2,1)S(1)}, bf16[2,256,256]{2,1,0:T(8,128)(2,1)S(1)}, u32[]{:S(2)}, u32[]{:S(2)}) %collective-permute-start.23) | collective-permute-done | bytes 262176 | tf_op jit(solution)/shard_map/ppermute | solution.py:28
  261.2 3.7 %collective-permute-start.24 = (bf16[256,256]{1,0:T(8,128)(2,1)S(1)}, bf16[256,256]{1,0:T(8,128)(2,1)S(1)}, u32[]{:S(2)}, u32[]{:S(2)}) collective-permute-start(bf16[256,256]{1,0:T(8,128)(2,1)S(1)} %get-tuple-element.45), channel_id=1, source_target_pairs={{0,0},{1,1},{2,2},{3,3},{4,4},{5,5},{6,6},{7,7},{8,128},{9,129},{1... | collective-permute-start | bytes 393224 | tf_op jit(solution)/shard_map/ppermute | solution.py:28
  (101 shorter events, 68.3 us)
Async XLA Ops:
  6.5 141.3 %all-gather.5.cloned.1.call-start = ((), (), s32[]{:S(2)}) async-start(), calls=%async_computation | async-start | bytes 8912896 | tf_op jit(solution)/shard_map/all_gather | solution.py:86
  7.3 172.9 %all-gather.7.cloned.1.call-start = ((), (), s32[]{:S(2)}) async-start(), calls=%async_computation.1 | async-start | bytes 4718592 | tf_op jit(solution)/shard_map/all_gather | solution.py:73
  8.8 21.7 %collective-permute-start = (bf16[3,512,512]{2,1,0:T(8,128)(2,1)S(1)}, bf16[3,512,512]{2,1,0:T(8,128)(2,1)S(1)}, u32[]{:S(2)}, u32[]{:S(2)}) collective-permute-start(bf16[3,512,512]{2,1,0:T(8,128)(2,1)S(1)} %pad_maximum_fusion), channel_id=1, source_target_pairs={{0,0},{1,17},{2,2},{3,19},{4,4},{5,21},{6,6},{7,23},{8,1},{9,16},{... | collective-permute-start | bytes 4718600 | tf_op jit(solution)/shard_map/ppermute | solution.py:28
  31.4 191.6 %all-gather.9.cloned.1.call-start = ((), (), s32[]{:S(2)}) async-start(), calls=%async_computation.2 | async-start | bytes 4718592 | tf_op jit(solution)/shard_map/all_gather | solution.py:73
  31.5 27.0 %collective-permute-start.4 = (bf16[2,512,512]{2,1,0:T(8,128)(2,1)S(1)}, bf16[2,512,512]{2,1,0:T(8,128)(2,1)S(1)}, u32[]{:S(2)}, u32[]{:S(2)}) collective-permute-start(bf16[2,512,512]{2,1,0:T(8,128)(2,1)S(1)} %slice.32.refs_0_), channel_id=1, source_target_pairs={{0,1},{1,2},{2,3},{3,4},{4,5},{5,6},{6,7},{7,0},{8,9},{9,10},{10,1... | collective-permute-start | bytes 3145736 | tf_op jit(solution)/shard_map/ppermute | solution.py:28
  34.6 25.1 %collective-permute-start.1 = (bf16[2,512,512]{2,1,0:T(8,128)(2,1)S(1)}, bf16[2,512,512]{2,1,0:T(8,128)(2,1)S(1)}, u32[]{:S(2)}, u32[]{:S(2)}) collective-permute-start(bf16[2,512,512]{2,1,0:T(8,128)(2,1)S(1)} %slice.32.refs_0_), channel_id=1, source_target_pairs={{0,7},{1,0},{2,1},{3,2},{4,3},{5,4},{6,5},{7,6},{8,15},{9,8},{10,9... | collective-permute-start | bytes 3145736 | tf_op jit(solution)/shard_map/ppermute | solution.py:28
  58.5 25.3 %collective-permute-start.5 = (bf16[2,512,512]{2,1,0:T(8,128)(2,1)S(1)}, bf16[2,512,512]{2,1,0:T(8,128)(2,1)}, u32[]{:S(2)}, u32[]{:S(2)}) collective-permute-start(bf16[2,512,512]{2,1,0:T(8,128)(2,1)S(1)} %collective-permute-done.4.refs_8_), channel_id=1, source_target_pairs={{0,1},{1,2},{2,3},{3,4},{4,5},{5,6},{6,7},{7,0},{8,9},{9,10},{10,1... | collective-permute-start | bytes 3145736 | tf_op jit(solution)/shard_map/ppermute | solution.py:28
  59.7 25.5 %collective-permute-start.2 = (bf16[2,512,512]{2,1,0:T(8,128)(2,1)S(1)}, bf16[2,512,512]{2,1,0:T(8,128)(2,1)}, u32[]{:S(2)}, u32[]{:S(2)}) collective-permute-start(bf16[2,512,512]{2,1,0:T(8,128)(2,1)S(1)} %collective-permute-done.1.refs_1_), channel_id=1, source_target_pairs={{0,7},{1,0},{2,1},{3,2},{4,3},{5,4},{6,5},{7,6},{8,15},{9,8},{10,9... | collective-permute-start | bytes 3145736 | tf_op jit(solution)/shard_map/ppermute | solution.py:28
  64.5 24.1 %collective-permute-start.15 = (bf16[512,512]{1,0:T(8,128)(2,1)}, bf16[512,512]{1,0:T(8,128)(2,1)}, u32[]{:S(2)}, u32[]{:S(2)}) collective-permute-start(bf16[512,512]{1,0:T(8,128)(2,1)} %param.15), channel_id=1, source_target_pairs={{0,0},{1,16},{2,2},{3,18},{4,4},{5,20},{6,6},{7,22},{8,8},{9,24},{... | collective-permute-start | bytes 1572872 | tf_op jit(solution)/shard_map/ppermute | solution.py:28
  83.8 27.9 %collective-permute-start.6 = (bf16[2,512,512]{2,1,0:T(8,128)(2,1)}, bf16[2,512,512]{2,1,0:T(8,128)(2,1)S(1)}, u32[]{:S(2)}, u32[]{:S(2)}) collective-permute-start(bf16[2,512,512]{2,1,0:T(8,128)(2,1)} %collective-permute-done.5.refs_7_), channel_id=1, source_target_pairs={{0,1},{1,2},{2,3},{3,4},{4,5},{5,6},{6,7},{7,0},{8,9},{9,10},{10,1... | collective-permute-start | bytes 3145736 | tf_op jit(solution)/shard_map/ppermute | solution.py:28
  85.2 36.0 %collective-permute-start.3 = (bf16[2,512,512]{2,1,0:T(8,128)(2,1)}, bf16[2,512,512]{2,1,0:T(8,128)(2,1)S(1)}, u32[]{:S(2)}, u32[]{:S(2)}) collective-permute-start(bf16[2,512,512]{2,1,0:T(8,128)(2,1)} %collective-permute-done.2.refs_2_), channel_id=1, source_target_pairs={{0,7},{1,0},{2,1},{3,2},{4,3},{5,4},{6,5},{7,6},{8,15},{9,8},{10,9... | collective-permute-start | bytes 3145736 | tf_op jit(solution)/shard_map/ppermute | solution.py:28
  112.5 30.2 %collective-permute-start.7 = (bf16[1,512,512]{2,1,0:T(8,128)(2,1)}, bf16[1,512,512]{2,1,0:T(8,128)(2,1)}, u32[]{:S(2)}, u32[]{:S(2)}) collective-permute-start(bf16[1,512,512]{2,1,0:T(8,128)(2,1)} %slice.33), channel_id=1, source_target_pairs={{0,1},{1,2},{2,3},{3,4},{4,5},{5,6},{6,7},{7,0},{8,9},{9,10},{10,1... | collective-permute-start | bytes 1572872 | tf_op jit(solution)/shard_map/ppermute | solution.py:28
  122.1 25.8 %collective-permute-start.8 = (bf16[1,512,512]{2,1,0:T(8,128)(2,1)}, bf16[1,512,512]{2,1,0:T(8,128)(2,1)}, u32[]{:S(2)}, u32[]{:S(2)}) collective-permute-start(bf16[1,512,512]{2,1,0:T(8,128)(2,1)} %slice.34), channel_id=1, source_target_pairs={{0,7},{1,0},{2,1},{3,2},{4,3},{5,4},{6,5},{7,6},{8,15},{9,8},{10,9... | collective-permute-start | bytes 1572872 | tf_op jit(solution)/shard_map/ppermute | solution.py:28
  137.3 42.9 %collective-permute-start.10 = (bf16[256,4096]{1,0:T(8,128)(2,1)}, bf16[256,4096]{1,0:T(8,128)(2,1)}, u32[]{:S(2)}, u32[]{:S(2)}) collective-permute-start(bf16[256,4096]{1,0:T(8,128)(2,1)} %dynamic-slice_bitcast_fusion), channel_id=1, source_target_pairs={{0,8},{1,9},{2,10},{3,11},{4,12},{5,13},{6,14},{7,15},{8,0},{9,1},... | collective-permute-start | bytes 6291464 | tf_op jit(solution)/shard_map/ppermute | solution.py:28
  170.3 21.5 %collective-permute-start.9 = (f32[2,512,512]{2,1,0:T(8,128)}, f32[2,512,512]{2,1,0:T(8,128)}, u32[]{:S(2)}, u32[]{:S(2)}) collective-permute-start(f32[2,512,512]{2,1,0:T(8,128)} %get-tuple-element.24), channel_id=1, source_target_pairs={{0,16},{1,17},{2,18},{3,19},{4,20},{5,21},{6,22},{7,23},{8,24},{9,... | collective-permute-start | bytes 6291464 | tf_op jit(solution)/shard_map/ppermute | solution.py:28
  207.4 15.6 %collective-permute-start.14 = (bf16[2,256,512]{2,1,0:T(8,128)(2,1)S(1)}, bf16[2,256,512]{2,1,0:T(8,128)(2,1)S(1)}, u32[]{:S(2)}, u32[]{:S(2)}) collective-permute-start(bf16[2,256,512]{2,1,0:T(8,128)(2,1)S(1)} %pad_maximum_fusion.1.mine_ref), channel_id=1, source_target_pairs={{0,16},{1,17},{2,18},{3,19},{4,20},{5,21},{6,22},{7,23},{8,24},{9,... | collective-permute-start | bytes 1572872 | tf_op jit(solution)/shard_map/ppermute | solution.py:28
  228.8 9.7 %collective-permute-start.16 = (bf16[2,256,256]{2,1,0:T(8,128)(2,1)S(1)}, bf16[2,256,256]{2,1,0:T(8,128)(2,1)S(1)}, u32[]{:S(2)}, u32[]{:S(2)}) collective-permute-start(bf16[2,256,256]{2,1,0:T(8,128)(2,1)S(1)} %get-tuple-element.34), channel_id=1, source_target_pairs={{0,64},{1,65},{2,66},{3,67},{4,68},{5,69},{6,70},{7,71},{8,72},{9,... | collective-permute-start | bytes 786440 | tf_op jit(solution)/shard_map/ppermute | solution.py:28
  230.4 15.5 %collective-permute-start.17 = (bf16[2,256,256]{2,1,0:T(8,128)(2,1)S(1)}, bf16[2,256,256]{2,1,0:T(8,128)(2,1)S(1)}, u32[]{:S(2)}, u32[]{:S(2)}) collective-permute-start(bf16[2,256,256]{2,1,0:T(8,128)(2,1)S(1)} %get-tuple-element.35), channel_id=1, source_target_pairs={{0,128},{1,129},{2,130},{3,131},{4,132},{5,133},{6,134},{7,135},{8... | collective-permute-start | bytes 786440 | tf_op jit(solution)/shard_map/ppermute | solution.py:28
  233.1 16.1 %collective-permute-start.18 = (bf16[2,256,256]{2,1,0:T(8,128)(2,1)S(1)}, bf16[2,256,256]{2,1,0:T(8,128)(2,1)S(1)}, u32[]{:S(2)}, u32[]{:S(2)}) collective-permute-start(bf16[2,256,256]{2,1,0:T(8,128)(2,1)S(1)} %get-tuple-element.36), channel_id=1, source_target_pairs={{0,192},{1,193},{2,194},{3,195},{4,196},{5,197},{6,198},{7,199},{8... | collective-permute-start | bytes 786440 | tf_op jit(solution)/shard_map/ppermute | solution.py:28
  234.3 22.1 %collective-permute-start.21 = (bf16[2,256,256]{2,1,0:T(8,128)(2,1)S(1)}, bf16[2,256,256]{2,1,0:T(8,128)(2,1)S(1)}, u32[]{:S(2)}, u32[]{:S(2)}) collective-permute-start(bf16[2,256,256]{2,1,0:T(8,128)(2,1)S(1)} %get-tuple-element.38), channel_id=1, source_target_pairs={{0,64},{1,65},{2,66},{3,67},{4,68},{5,69},{6,70},{7,71},{8,72},{9,... | collective-permute-start | bytes 786440 | tf_op jit(solution)/shard_map/ppermute | solution.py:28
  234.7 21.7 %collective-permute-start.22 = (bf16[2,256,256]{2,1,0:T(8,128)(2,1)S(1)}, bf16[2,256,256]{2,1,0:T(8,128)(2,1)S(1)}, u32[]{:S(2)}, u32[]{:S(2)}) collective-permute-start(bf16[2,256,256]{2,1,0:T(8,128)(2,1)S(1)} %get-tuple-element.39), channel_id=1, source_target_pairs={{0,128},{1,129},{2,130},{3,131},{4,132},{5,133},{6,134},{7,135},{8... | collective-permute-start | bytes 786440 | tf_op jit(solution)/shard_map/ppermute | solution.py:28
  238.6 22.5 %collective-permute-start.23 = (bf16[2,256,256]{2,1,0:T(8,128)(2,1)S(1)}, bf16[2,256,256]{2,1,0:T(8,128)(2,1)S(1)}, u32[]{:S(2)}, u32[]{:S(2)}) collective-permute-start(bf16[2,256,256]{2,1,0:T(8,128)(2,1)S(1)} %get-tuple-element.40), channel_id=1, source_target_pairs={{0,192},{1,193},{2,194},{3,195},{4,196},{5,197},{6,198},{7,199},{8... | collective-permute-start | bytes 786440 | tf_op jit(solution)/shard_map/ppermute | solution.py:28
  249.3 19.0 %collective-permute-start.19 = (bf16[256,256]{1,0:T(8,128)(2,1)S(1)}, bf16[256,256]{1,0:T(8,128)(2,1)S(1)}, u32[]{:S(2)}, u32[]{:S(2)}) collective-permute-start(bf16[256,256]{1,0:T(8,128)(2,1)S(1)} %get-tuple-element.43), channel_id=1, source_target_pairs={{0,0},{1,1},{2,2},{3,3},{4,4},{5,5},{6,6},{7,7},{8,128},{9,129},{1... | collective-permute-start | bytes 393224 | tf_op jit(solution)/shard_map/ppermute | solution.py:28
  251.2 17.1 %collective-permute-start.20 = (bf16[256,256]{1,0:T(8,128)(2,1)S(1)}, bf16[256,256]{1,0:T(8,128)(2,1)S(1)}, u32[]{:S(2)}, u32[]{:S(2)}) collective-permute-start(bf16[256,256]{1,0:T(8,128)(2,1)S(1)} %get-tuple-element.44), channel_id=1, source_target_pairs={{0,32},{1,33},{2,34},{3,35},{4,36},{5,37},{6,38},{7,39},{8,160},{9... | collective-permute-start | bytes 393224 | tf_op jit(solution)/shard_map/ppermute | solution.py:28
  (20 other events, 201.4 us)
Sparse Core Ops, SparseCore 0:
  9.8 83.0 all-gather.4
  94.7 69.6 all-gather.6
  166.2 56.7 all-gather.8

commit v4 on v3

--- a/solution.py
+++ b/solution.py
@@ -203,7 +203,7 @@
 
 def out_kernel(place_ref, mine_ref, theirs_ref, near_ref, far_ref, *parts):
     core, x_high = place_ref[2], place_ref[0] // 2
-    cut = near_ref.shape[1] // 2
+    cut = parts[0].shape[1]
 
     def product(ref):
         return (
@@ -219,7 +219,7 @@
         @pl.when(pl.program_id(0) // 2 == n)
         def _():
             for half in range(2):
-                columns = slice(half * cut, (half + 1) * cut)
+                columns = slice(cut, None) if half else slice(0, cut)
                 parts[4 * half + n][...] = near[:, columns]
                 parts[4 * half + 2 + n][...] = far[:, columns]
 
@@ -236,20 +236,22 @@
 
         return pl.BlockSpec((None, depth, width), index)
 
-    def out_spec(n):
+    cuts = [3 * width // 4] * 4 + [width // 4] * 4
+
+    def out_spec(n, cut):
         def index(s, p):
             return (jnp.where(s // 2 == n, s % 2, jnp.where(s // 2 < n, 0, 1)), 0, 0)
 
-        return pl.BlockSpec((None, length, width // 2), index)
+        return pl.BlockSpec((None, length, cut), index)
 
     return pl.pallas_call(
         out_kernel,
-        out_shape=[jax.ShapeDtypeStruct((2, length, width // 2), jnp.bfloat16)] * 8,
+        out_shape=[jax.ShapeDtypeStruct((2, length, cut), jnp.bfloat16) for cut in cuts],
         grid_spec=pltpu.PrefetchScalarGridSpec(
             num_scalar_prefetch=1,
             grid=(steps,),
             in_specs=[rows, rows, block_spec(0), block_spec(1)],
-            out_specs=[out_spec(n % 2) for n in range(8)],
+            out_specs=[out_spec(n % 2, cut) for n, cut in enumerate(cuts)],
         ),
         compiler_params=pltpu.CompilerParams(vmem_limit_bytes=16 * 2**20),
         cost_estimate=pl.CostEstimate(

time: 283 us -> 283 us (level)
  transfers between devices with their start and end apart: 29 -> 29, of which waited for: 16 -> 17; matrix products, arithmetic and copies ran while one was open for 5% -> 5% of each run, Pallas kernels for 10% -> 10%
where the time goes in v4:
time: 283 us; the launch traced here: 281 us
  waiting for transfers between devices  143 us (51%)
  starting transfers between devices  59.1 us (21%)
  Pallas kernels  30.4 us (11%)
  local copies, waits for them, and re-layouts  25 us (9%)
  between operations  14.1 us (5%)
  other arithmetic  6.78 us (2%)
    ppermute x26, waiting for transfers between devices, permute(): return lax.ppermute(value, AXES, pairs)  127 us
    ppermute x26, starting transfers between devices, permute(): return lax.ppermute(value, AXES, pairs)  59 us
    unnamed x30, local copies, waits for them, and re-layouts  18.9 us
    all_gather x2, waiting for transfers between devices, gather_z(): return lax.all_gather(value, 'fsdp', axis=0, axis_index_groups=groups)  15.5 us
    pallas_call x1, Pallas kernels, project_latents(): pl.pallas_call(latent_kernel, out_shape=(out, out), grid_spec=pltpu.Prefe...  15.2 us
    pallas_call x1, Pallas kernels, project_queries(): pl.pallas_call(query_kernel, out_shape=(out, out), grid_spec=pltpu.Prefet...  7.07 us
  transfers between devices with their start and end apart: 29, of which 17 were waited for; matrix products, arithmetic and copies ran while one was open for 5% of the time, Pallas kernels for 10%

profile of v4, /device:TPU:8, one launch (start us, length us, event | category | flops | bytes accessed | tf_op | source)
XLA Modules:
  0.0 280.9 jit_solution(12706328548667816848)
XLA Ops:
  8.8 3.7 %collective-permute-start = (bf16[3,512,512]{2,1,0:T(8,128)(2,1)S(1)}, bf16[3,512,512]{2,1,0:T(8,128)(2,1)S(1)}, u32[]{:S(2)}, u32[]{:S(2)}) collective-permute-start(bf16[3,512,512]{2,1,0:T(8,128)(2,1)S(1)} %pad_maximum_fusion), channel_id=1, source_target_pairs={{0,0},{1,17},{2,2},{3,19},{4,4},{5,21},{6,6},{7,23},{8,1},{9,16},{... | collective-permute-start | bytes 4718600 | tf_op jit(solution)/shard_map/ppermute | solution.py:28
  12.6 18.0 %collective-permute-done = bf16[3,512,512]{2,1,0:T(8,128)(2,1)S(1)} collective-permute-done((bf16[3,512,512]{2,1,0:T(8,128)(2,1)S(1)}, bf16[3,512,512]{2,1,0:T(8,128)(2,1)S(1)}, u32[]{:S(2)}, u32[]{:S(2)}) %collective-permute-start) | collective-permute-done | bytes 1572896 | tf_op jit(solution)/shard_map/ppermute | solution.py:28
  34.6 4.0 %collective-permute-start.1 = (bf16[2,512,512]{2,1,0:T(8,128)(2,1)S(1)}, bf16[2,512,512]{2,1,0:T(8,128)(2,1)S(1)}, u32[]{:S(2)}, u32[]{:S(2)}) collective-permute-start(bf16[2,512,512]{2,1,0:T(8,128)(2,1)S(1)} %slice.32.refs_0_), channel_id=1, source_target_pairs={{0,7},{1,0},{2,1},{3,2},{4,3},{5,4},{6,5},{7,6},{8,15},{9,8},{10,9... | collective-permute-start | bytes 3145736 | tf_op jit(solution)/shard_map/ppermute | solution.py:28
  38.6 19.9 %collective-permute-done.4.refs_8_ = bf16[2,512,512]{2,1,0:T(8,128)(2,1)S(1)} collective-permute-done((bf16[2,512,512]{2,1,0:T(8,128)(2,1)S(1)}, bf16[2,512,512]{2,1,0:T(8,128)(2,1)S(1)}, u32[]{:S(2)}, u32[]{:S(2)}) %collective-permute-start.4) | collective-permute-done | bytes 1048608 | tf_op jit(solution)/shard_map/ppermute | solution.py:28
  59.7 3.8 %collective-permute-start.2 = (bf16[2,512,512]{2,1,0:T(8,128)(2,1)S(1)}, bf16[2,512,512]{2,1,0:T(8,128)(2,1)}, u32[]{:S(2)}, u32[]{:S(2)}) collective-permute-start(bf16[2,512,512]{2,1,0:T(8,128)(2,1)S(1)} %collective-permute-done.1.refs_1_), channel_id=1, source_target_pairs={{0,7},{1,0},{2,1},{3,2},{4,3},{5,4},{6,5},{7,6},{8,15},{9,8},{10,9... | collective-permute-start | bytes 3145736 | tf_op jit(solution)/shard_map/ppermute | solution.py:28
  64.5 5.4 %collective-permute-start.15 = (bf16[512,512]{1,0:T(8,128)(2,1)}, bf16[512,512]{1,0:T(8,128)(2,1)}, u32[]{:S(2)}, u32[]{:S(2)}) collective-permute-start(bf16[512,512]{1,0:T(8,128)(2,1)} %param.15), channel_id=1, source_target_pairs={{0,0},{1,16},{2,2},{3,18},{4,4},{5,20},{6,6},{7,22},{8,8},{9,24},{... | collective-permute-start | bytes 1572872 | tf_op jit(solution)/shard_map/ppermute | solution.py:28
  69.9 13.9 %collective-permute-done.5.refs_7_ = bf16[2,512,512]{2,1,0:T(8,128)(2,1)} collective-permute-done((bf16[2,512,512]{2,1,0:T(8,128)(2,1)S(1)}, bf16[2,512,512]{2,1,0:T(8,128)(2,1)}, u32[]{:S(2)}, u32[]{:S(2)}) %collective-permute-start.5) | collective-permute-done | bytes 1048608 | tf_op jit(solution)/shard_map/ppermute | solution.py:28
  88.6 23.1 %collective-permute-done.6.refs_6_ = bf16[2,512,512]{2,1,0:T(8,128)(2,1)S(1)} collective-permute-done((bf16[2,512,512]{2,1,0:T(8,128)(2,1)}, bf16[2,512,512]{2,1,0:T(8,128)(2,1)S(1)}, u32[]{:S(2)}, u32[]{:S(2)}) %collective-permute-start.6) | collective-permute-done | bytes 1048608 | tf_op jit(solution)/shard_map/ppermute | solution.py:28
  114.9 6.3 %collective-permute-done.3.refs_3_ = bf16[2,512,512]{2,1,0:T(8,128)(2,1)S(1)} collective-permute-done((bf16[2,512,512]{2,1,0:T(8,128)(2,1)}, bf16[2,512,512]{2,1,0:T(8,128)(2,1)S(1)}, u32[]{:S(2)}, u32[]{:S(2)}) %collective-permute-start.3) | collective-permute-done | bytes 1048608 | tf_op jit(solution)/shard_map/ppermute | solution.py:28
  122.1 5.8 %collective-permute-start.8 = (bf16[1,512,512]{2,1,0:T(8,128)(2,1)}, bf16[1,512,512]{2,1,0:T(8,128)(2,1)}, u32[]{:S(2)}, u32[]{:S(2)}) collective-permute-start(bf16[1,512,512]{2,1,0:T(8,128)(2,1)} %slice.34), channel_id=1, source_target_pairs={{0,7},{1,0},{2,1},{3,2},{4,3},{5,4},{6,5},{7,6},{8,15},{9,8},{10,9... | collective-permute-start | bytes 1572872 | tf_op jit(solution)/shard_map/ppermute | solution.py:28
  130.2 4.4 %shard_map.92.own_ref = bf16[2,256,4096]{2,1,0:T(8,128)(2,1)S(1)} custom-call(bf16[256,8192]{1,0:T(8,128)(2,1)S(1)} %bitcast.46, f32[1,8192]{1,0:T(1,128)S(1)} %bitcast.47), custom_call_target="tpu_custom_call" | custom-call | flops 16777216 | bytes 8388608 | tf_op jit(solution)/shard_map/pallas_call | solution.py:278
  138.4 4.3 %collective-permute-done.7.refs_4_ = bf16[1,512,512]{2,1,0:T(8,128)(2,1)} collective-permute-done((bf16[1,512,512]{2,1,0:T(8,128)(2,1)}, bf16[1,512,512]{2,1,0:T(8,128)(2,1)}, u32[]{:S(2)}, u32[]{:S(2)}) %collective-permute-start.7) | collective-permute-done | bytes 524320 | tf_op jit(solution)/shard_map/ppermute | solution.py:28
  142.7 5.1 %collective-permute-done.8.refs_5_ = bf16[1,512,512]{2,1,0:T(8,128)(2,1)} collective-permute-done((bf16[1,512,512]{2,1,0:T(8,128)(2,1)}, bf16[1,512,512]{2,1,0:T(8,128)(2,1)}, u32[]{:S(2)}, u32[]{:S(2)}) %collective-permute-start.8) | collective-permute-done | bytes 524320 | tf_op jit(solution)/shard_map/ppermute | solution.py:28
  153.8 15.2 %shard_map.91 = (f32[2,512,512]{2,1,0:T(8,128)S(1)}, f32[2,512,512]{2,1,0:T(8,128)}) custom-call(s32[5]{0:T(128)S(1)} %stack.41.place_ref, bf16[16,512,512]{2,1,0:T(8,128)(2,1)S(1)} %copy-done, bf16[16,512,512]{2,1,0:T(8,128)(2,1)S(1)} %copy-done, bf16[16,512,512]{2,1,0:T(8,128)(2,1)S(1)} %copy-done, bf16[16,512,512]{2,1,0:T(8,128)(2,1)S(1)} %copy-done, ...), custom_call_target="tpu_custom_call" | custom-call | flops 8589934592 | bytes 20971520 | tf_op jit(solution)/shard_map/pallas_call | solution.py:180
  171.1 8.7 %collective-permute-done.11 = s32[1,256]{1,0:T(1,128)S(1)} collective-permute-done((s32[1,256]{1,0:T(1,128)S(1)}, s32[1,256]{1,0:T(1,128)S(1)}, u32[]{:S(2)}, u32[]{:S(2)}) %collective-permute-start.11) | collective-permute-done | bytes 1056 | tf_op jit(solution)/shard_map/ppermute | solution.py:28
  184.6 7.1 %shard_map.93 = (f32[256,512]{1,0:T(8,128)S(1)}, f32[256,512]{1,0:T(8,128)S(1)}) custom-call(s32[5]{0:T(128)S(1)} %stack.41.place_ref, bf16[2,256,4096]{2,1,0:T(8,128)(2,1)S(1)} %copy-done.2, bf16[256,4096]{1,0:T(8,128)(2,1)} %collective-permute-done.10.other_ref, bf16[8,512,512]{2,1,0:T(8,128)(2,1)S(1)} %copy-done.5), custom_call_target="tpu_custom_call" | custom-call | flops 2147483648 | bytes 9437184 | tf_op jit(solution)/shard_map/pallas_call | solution.py:145
  199.3 8.1 %collective-permute-done.13 = bf16[256,512]{1,0:T(8,128)(2,1)S(1)} collective-permute-done((bf16[256,512]{1,0:T(8,128)(2,1)S(1)}, bf16[256,512]{1,0:T(8,128)(2,1)S(1)}, u32[]{:S(2)}, u32[]{:S(2)}) %collective-permute-start.13) | collective-permute-done | bytes 262176 | tf_op jit(solution)/shard_map/ppermute | solution.py:28
  207.5 15.5 %all-gather.9.cloned.1.call-done = bf16[4096,512]{1,0:T(8,128)(2,1)} async-done(((bf16[512,512]{1,0:T(8,128)(2,1)}), bf16[4096,512]{1,0:T(8,128)(2,1)}) %all-gather.9.cloned.1.call-update) | async-done | bytes 4194320 | tf_op jit(solution)/shard_map/all_gather | solution.py:73
  225.2 3.7 %shard_map.94 = (bf16[2,256,384]{2,1,0:T(8,128)(2,1)S(1)}, bf16[2,256,384]{2,1,0:T(8,128)(2,1)S(1)}, bf16[2,256,384]{2,1,0:T(8,128)(2,1)S(1)}, bf16[2,256,384]{2...) custom-call(s32[5]{0:T(128)S(1)} %stack.41.place_ref, ...), custom_call_target="tpu_custom_call" | custom-call | flops 2147483648 | bytes 7340032 | tf_op jit(solution)/shard_map/pallas_call | solution.py:247
  234.7 3.9 %collective-permute-start.17 = (bf16[2,256,384]{2,1,0:T(8,128)(2,1)S(1)}, bf16[2,256,384]{2,1,0:T(8,128)(2,1)S(1)}, u32[]{:S(2)}, u32[]{:S(2)}) collective-permute-start(bf16[2,256,384]{2,1,0:T(8,128)(2,1)S(1)} %get-tuple-element.35), channel_id=1, source_target_pairs={{0,128},{1,129},{2,130},{3,131},{4,132},{5,133},{6,134},{7,135},{8... | collective-permute-start | bytes 1179656 | tf_op jit(solution)/shard_map/ppermute | solution.py:28
  244.3 4.6 %collective-permute-start.25 = (bf16[256,128]{1,0:T(8,128)(2,1)S(1)}, bf16[256,128]{1,0:T(8,128)(2,1)S(1)}, u32[]{:S(2)}, u32[]{:S(2)}) collective-permute-start(bf16[256,128]{1,0:T(8,128)(2,1)S(1)} %get-tuple-element.46), channel_id=1, source_target_pairs={{0,32},{1,33},{2,34},{3,35},{4,36},{5,37},{6,38},{7,39},{8,160},{9... | collective-permute-start | bytes 196616 | tf_op jit(solution)/shard_map/ppermute | solution.py:28
  248.9 7.2 %collective-permute-done.17 = bf16[2,256,384]{2,1,0:T(8,128)(2,1)S(1)} collective-permute-done((bf16[2,256,384]{2,1,0:T(8,128)(2,1)S(1)}, bf16[2,256,384]{2,1,0:T(8,128)(2,1)S(1)}, u32[]{:S(2)}, u32[]{:S(2)}) %collective-permute-start.17) | collective-permute-done | bytes 393248 | tf_op jit(solution)/shard_map/ppermute | solution.py:28
  258.4 3.8 %collective-permute-start.19 = (bf16[256,384]{1,0:T(8,128)(2,1)S(1)}, bf16[256,384]{1,0:T(8,128)(2,1)S(1)}, u32[]{:S(2)}, u32[]{:S(2)}) collective-permute-start(bf16[256,384]{1,0:T(8,128)(2,1)S(1)} %get-tuple-element.43), channel_id=1, source_target_pairs={{0,0},{1,1},{2,2},{3,3},{4,4},{5,5},{6,6},{7,7},{8,128},{9,129},{1... | collective-permute-start | bytes 589832 | tf_op jit(solution)/shard_map/ppermute | solution.py:28
  269.0 3.6 %collective-permute-done.20 = bf16[256,384]{1,0:T(8,128)(2,1)S(1)} collective-permute-done((bf16[256,384]{1,0:T(8,128)(2,1)S(1)}, bf16[256,384]{1,0:T(8,128)(2,1)S(1)}, u32[]{:S(2)}, u32[]{:S(2)}) %collective-permute-start.20) | collective-permute-done | bytes 196640 | tf_op jit(solution)/shard_map/ppermute | solution.py:28
  (101 shorter events, 67.6 us)
Async XLA Ops:
  6.5 141.3 %all-gather.5.cloned.1.call-start = ((), (), s32[]{:S(2)}) async-start(), calls=%async_computation | async-start | bytes 8912896 | tf_op jit(solution)/shard_map/all_gather | solution.py:86
  7.3 172.9 %all-gather.7.cloned.1.call-start = ((), (), s32[]{:S(2)}) async-start(), calls=%async_computation.1 | async-start | bytes 4718592 | tf_op jit(solution)/shard_map/all_gather | solution.py:73
  8.8 21.7 %collective-permute-start = (bf16[3,512,512]{2,1,0:T(8,128)(2,1)S(1)}, bf16[3,512,512]{2,1,0:T(8,128)(2,1)S(1)}, u32[]{:S(2)}, u32[]{:S(2)}) collective-permute-start(bf16[3,512,512]{2,1,0:T(8,128)(2,1)S(1)} %pad_maximum_fusion), channel_id=1, source_target_pairs={{0,0},{1,17},{2,2},{3,19},{4,4},{5,21},{6,6},{7,23},{8,1},{9,16},{... | collective-permute-start | bytes 4718600 | tf_op jit(solution)/shard_map/ppermute | solution.py:28
  31.4 191.6 %all-gather.9.cloned.1.call-start = ((), (), s32[]{:S(2)}) async-start(), calls=%async_computation.2 | async-start | bytes 4718592 | tf_op jit(solution)/shard_map/all_gather | solution.py:73
  31.5 27.0 %collective-permute-start.4 = (bf16[2,512,512]{2,1,0:T(8,128)(2,1)S(1)}, bf16[2,512,512]{2,1,0:T(8,128)(2,1)S(1)}, u32[]{:S(2)}, u32[]{:S(2)}) collective-permute-start(bf16[2,512,512]{2,1,0:T(8,128)(2,1)S(1)} %slice.32.refs_0_), channel_id=1, source_target_pairs={{0,1},{1,2},{2,3},{3,4},{4,5},{5,6},{6,7},{7,0},{8,9},{9,10},{10,1... | collective-permute-start | bytes 3145736 | tf_op jit(solution)/shard_map/ppermute | solution.py:28
  34.6 25.1 %collective-permute-start.1 = (bf16[2,512,512]{2,1,0:T(8,128)(2,1)S(1)}, bf16[2,512,512]{2,1,0:T(8,128)(2,1)S(1)}, u32[]{:S(2)}, u32[]{:S(2)}) collective-permute-start(bf16[2,512,512]{2,1,0:T(8,128)(2,1)S(1)} %slice.32.refs_0_), channel_id=1, source_target_pairs={{0,7},{1,0},{2,1},{3,2},{4,3},{5,4},{6,5},{7,6},{8,15},{9,8},{10,9... | collective-permute-start | bytes 3145736 | tf_op jit(solution)/shard_map/ppermute | solution.py:28
  58.5 25.3 %collective-permute-start.5 = (bf16[2,512,512]{2,1,0:T(8,128)(2,1)S(1)}, bf16[2,512,512]{2,1,0:T(8,128)(2,1)}, u32[]{:S(2)}, u32[]{:S(2)}) collective-permute-start(bf16[2,512,512]{2,1,0:T(8,128)(2,1)S(1)} %collective-permute-done.4.refs_8_), channel_id=1, source_target_pairs={{0,1},{1,2},{2,3},{3,4},{4,5},{5,6},{6,7},{7,0},{8,9},{9,10},{10,1... | collective-permute-start | bytes 3145736 | tf_op jit(solution)/shard_map/ppermute | solution.py:28
  59.7 25.5 %collective-permute-start.2 = (bf16[2,512,512]{2,1,0:T(8,128)(2,1)S(1)}, bf16[2,512,512]{2,1,0:T(8,128)(2,1)}, u32[]{:S(2)}, u32[]{:S(2)}) collective-permute-start(bf16[2,512,512]{2,1,0:T(8,128)(2,1)S(1)} %collective-permute-done.1.refs_1_), channel_id=1, source_target_pairs={{0,7},{1,0},{2,1},{3,2},{4,3},{5,4},{6,5},{7,6},{8,15},{9,8},{10,9... | collective-permute-start | bytes 3145736 | tf_op jit(solution)/shard_map/ppermute | solution.py:28
  64.5 24.1 %collective-permute-start.15 = (bf16[512,512]{1,0:T(8,128)(2,1)}, bf16[512,512]{1,0:T(8,128)(2,1)}, u32[]{:S(2)}, u32[]{:S(2)}) collective-permute-start(bf16[512,512]{1,0:T(8,128)(2,1)} %param.15), channel_id=1, source_target_pairs={{0,0},{1,16},{2,2},{3,18},{4,4},{5,20},{6,6},{7,22},{8,8},{9,24},{... | collective-permute-start | bytes 1572872 | tf_op jit(solution)/shard_map/ppermute | solution.py:28
  83.8 27.9 %collective-permute-start.6 = (bf16[2,512,512]{2,1,0:T(8,128)(2,1)}, bf16[2,512,512]{2,1,0:T(8,128)(2,1)S(1)}, u32[]{:S(2)}, u32[]{:S(2)}) collective-permute-start(bf16[2,512,512]{2,1,0:T(8,128)(2,1)} %collective-permute-done.5.refs_7_), channel_id=1, source_target_pairs={{0,1},{1,2},{2,3},{3,4},{4,5},{5,6},{6,7},{7,0},{8,9},{9,10},{10,1... | collective-permute-start | bytes 3145736 | tf_op jit(solution)/shard_map/ppermute | solution.py:28
  85.2 36.0 %collective-permute-start.3 = (bf16[2,512,512]{2,1,0:T(8,128)(2,1)}, bf16[2,512,512]{2,1,0:T(8,128)(2,1)S(1)}, u32[]{:S(2)}, u32[]{:S(2)}) collective-permute-start(bf16[2,512,512]{2,1,0:T(8,128)(2,1)} %collective-permute-done.2.refs_2_), channel_id=1, source_target_pairs={{0,7},{1,0},{2,1},{3,2},{4,3},{5,4},{6,5},{7,6},{8,15},{9,8},{10,9... | collective-permute-start | bytes 3145736 | tf_op jit(solution)/shard_map/ppermute | solution.py:28
  112.5 30.2 %collective-permute-start.7 = (bf16[1,512,512]{2,1,0:T(8,128)(2,1)}, bf16[1,512,512]{2,1,0:T(8,128)(2,1)}, u32[]{:S(2)}, u32[]{:S(2)}) collective-permute-start(bf16[1,512,512]{2,1,0:T(8,128)(2,1)} %slice.33), channel_id=1, source_target_pairs={{0,1},{1,2},{2,3},{3,4},{4,5},{5,6},{6,7},{7,0},{8,9},{9,10},{10,1... | collective-permute-start | bytes 1572872 | tf_op jit(solution)/shard_map/ppermute | solution.py:28
  122.1 25.8 %collective-permute-start.8 = (bf16[1,512,512]{2,1,0:T(8,128)(2,1)}, bf16[1,512,512]{2,1,0:T(8,128)(2,1)}, u32[]{:S(2)}, u32[]{:S(2)}) collective-permute-start(bf16[1,512,512]{2,1,0:T(8,128)(2,1)} %slice.34), channel_id=1, source_target_pairs={{0,7},{1,0},{2,1},{3,2},{4,3},{5,4},{6,5},{7,6},{8,15},{9,8},{10,9... | collective-permute-start | bytes 1572872 | tf_op jit(solution)/shard_map/ppermute | solution.py:28
  137.3 42.9 %collective-permute-start.10 = (bf16[256,4096]{1,0:T(8,128)(2,1)}, bf16[256,4096]{1,0:T(8,128)(2,1)}, u32[]{:S(2)}, u32[]{:S(2)}) collective-permute-start(bf16[256,4096]{1,0:T(8,128)(2,1)} %dynamic-slice_bitcast_fusion), channel_id=1, source_target_pairs={{0,8},{1,9},{2,10},{3,11},{4,12},{5,13},{6,14},{7,15},{8,0},{9,1},... | collective-permute-start | bytes 6291464 | tf_op jit(solution)/shard_map/ppermute | solution.py:28
  170.3 21.5 %collective-permute-start.9 = (f32[2,512,512]{2,1,0:T(8,128)}, f32[2,512,512]{2,1,0:T(8,128)}, u32[]{:S(2)}, u32[]{:S(2)}) collective-permute-start(f32[2,512,512]{2,1,0:T(8,128)} %get-tuple-element.24), channel_id=1, source_target_pairs={{0,16},{1,17},{2,18},{3,19},{4,20},{5,21},{6,22},{7,23},{8,24},{9,... | collective-permute-start | bytes 6291464 | tf_op jit(solution)/shard_map/ppermute | solution.py:28
  207.4 15.6 %collective-permute-start.14 = (bf16[2,256,512]{2,1,0:T(8,128)(2,1)S(1)}, bf16[2,256,512]{2,1,0:T(8,128)(2,1)S(1)}, u32[]{:S(2)}, u32[]{:S(2)}) collective-permute-start(bf16[2,256,512]{2,1,0:T(8,128)(2,1)S(1)} %pad_maximum_fusion.1.mine_ref), channel_id=1, source_target_pairs={{0,16},{1,17},{2,18},{3,19},{4,20},{5,21},{6,22},{7,23},{8,24},{9,... | collective-permute-start | bytes 1572872 | tf_op jit(solution)/shard_map/ppermute | solution.py:28
  228.9 9.7 %collective-permute-start.21 = (bf16[2,256,128]{2,1,0:T(8,128)(2,1)S(1)}, bf16[2,256,128]{2,1,0:T(8,128)(2,1)S(1)}, u32[]{:S(2)}, u32[]{:S(2)}) collective-permute-start(bf16[2,256,128]{2,1,0:T(8,128)(2,1)S(1)} %get-tuple-element.38), channel_id=1, source_target_pairs={{0,64},{1,65},{2,66},{3,67},{4,68},{5,69},{6,70},{7,71},{8,72},{9,... | collective-permute-start | bytes 393224 | tf_op jit(solution)/shard_map/ppermute | solution.py:28
  234.4 14.5 %collective-permute-start.16 = (bf16[2,256,384]{2,1,0:T(8,128)(2,1)S(1)}, bf16[2,256,384]{2,1,0:T(8,128)(2,1)S(1)}, u32[]{:S(2)}, u32[]{:S(2)}) collective-permute-start(bf16[2,256,384]{2,1,0:T(8,128)(2,1)S(1)} %get-tuple-element.34), channel_id=1, source_target_pairs={{0,64},{1,65},{2,66},{3,67},{4,68},{5,69},{6,70},{7,71},{8,72},{9,... | collective-permute-start | bytes 1179656 | tf_op jit(solution)/shard_map/ppermute | solution.py:28
  234.7 21.4 %collective-permute-start.17 = (bf16[2,256,384]{2,1,0:T(8,128)(2,1)S(1)}, bf16[2,256,384]{2,1,0:T(8,128)(2,1)S(1)}, u32[]{:S(2)}, u32[]{:S(2)}) collective-permute-start(bf16[2,256,384]{2,1,0:T(8,128)(2,1)S(1)} %get-tuple-element.35), channel_id=1, source_target_pairs={{0,128},{1,129},{2,130},{3,131},{4,132},{5,133},{6,134},{7,135},{8... | collective-permute-start | bytes 1179656 | tf_op jit(solution)/shard_map/ppermute | solution.py:28
  238.6 19.6 %collective-permute-start.18 = (bf16[2,256,384]{2,1,0:T(8,128)(2,1)S(1)}, bf16[2,256,384]{2,1,0:T(8,128)(2,1)S(1)}, u32[]{:S(2)}, u32[]{:S(2)}) collective-permute-start(bf16[2,256,384]{2,1,0:T(8,128)(2,1)S(1)} %get-tuple-element.36), channel_id=1, source_target_pairs={{0,192},{1,193},{2,194},{3,195},{4,196},{5,197},{6,198},{7,199},{8... | collective-permute-start | bytes 1179656 | tf_op jit(solution)/shard_map/ppermute | solution.py:28
  241.8 23.7 %collective-permute-start.24 = (bf16[256,128]{1,0:T(8,128)(2,1)S(1)}, bf16[256,128]{1,0:T(8,128)(2,1)S(1)}, u32[]{:S(2)}, u32[]{:S(2)}) collective-permute-start(bf16[256,128]{1,0:T(8,128)(2,1)S(1)} %get-tuple-element.45), channel_id=1, source_target_pairs={{0,0},{1,1},{2,2},{3,3},{4,4},{5,5},{6,6},{7,7},{8,128},{9,129},{1... | collective-permute-start | bytes 196616 | tf_op jit(solution)/shard_map/ppermute | solution.py:28
  244.3 21.2 %collective-permute-start.25 = (bf16[256,128]{1,0:T(8,128)(2,1)S(1)}, bf16[256,128]{1,0:T(8,128)(2,1)S(1)}, u32[]{:S(2)}, u32[]{:S(2)}) collective-permute-start(bf16[256,128]{1,0:T(8,128)(2,1)S(1)} %get-tuple-element.46), channel_id=1, source_target_pairs={{0,32},{1,33},{2,34},{3,35},{4,36},{5,37},{6,38},{7,39},{8,160},{9... | collective-permute-start | bytes 196616 | tf_op jit(solution)/shard_map/ppermute | solution.py:28
  258.4 10.5 %collective-permute-start.19 = (bf16[256,384]{1,0:T(8,128)(2,1)S(1)}, bf16[256,384]{1,0:T(8,128)(2,1)S(1)}, u32[]{:S(2)}, u32[]{:S(2)}) collective-permute-start(bf16[256,384]{1,0:T(8,128)(2,1)S(1)} %get-tuple-element.43), channel_id=1, source_target_pairs={{0,0},{1,1},{2,2},{3,3},{4,4},{5,5},{6,6},{7,7},{8,128},{9,129},{1... | collective-permute-start | bytes 589832 | tf_op jit(solution)/shard_map/ppermute | solution.py:28
  262.3 10.3 %collective-permute-start.20 = (bf16[256,384]{1,0:T(8,128)(2,1)S(1)}, bf16[256,384]{1,0:T(8,128)(2,1)S(1)}, u32[]{:S(2)}, u32[]{:S(2)}) collective-permute-start(bf16[256,384]{1,0:T(8,128)(2,1)S(1)} %get-tuple-element.44), channel_id=1, source_target_pairs={{0,32},{1,33},{2,34},{3,35},{4,36},{5,37},{6,38},{7,39},{8,160},{9... | collective-permute-start | bytes 589832 | tf_op jit(solution)/shard_map/ppermute | solution.py:28
  (20 other events, 202.5 us)
Sparse Core Ops, SparseCore 0:
  9.8 83.0 all-gather.4
  94.7 69.6 all-gather.6
  166.2 56.7 all-gather.8
